TPU v7x, 1024 devices: a whole 8x8x8 slice. The times are simulated.
1024 devices in a mesh: orb: 32 (over x, y_hi), bas: 32 (over y_lo, z, core).
Axes of the slice: x: 8, y: 8 (y_hi: 4, y_lo: 2; y = y_hi * 2 + y_lo), z: 8, core: 2. Of those that a mesh axis runs over, the one named last changes fastest.
Arguments:
- three_centre: bfloat16 [64, 32768, 256], P('bas', 'orb'), may hold values from -0.375 to 0.375
- occ_coeff: bfloat16 [512, 1024], P('orb'), may hold values from -1.5 to 1.5
- amp_coeff: bfloat16 [512, 1024], P('orb'), may hold values from -1.5 to 1.5
- col_blocks: int32 [32, 2], P('orb'), may hold values from 0 to 7, as said below
- slot_map: int32 [32, 64], P('orb'), may hold values from 0 to 63, as said below
- pair_list: int32 [32, 32, 32], P('orb', 'bas'), may hold values from 0 to 63, as said below
- pair_count: int32 [32, 32], P('orb', 'bas'), may hold values from 1 to 32, as said below
Outputs:
- exchange_blocks: float32 [32, 64, 128, 128], P('orb', 'bas')
Inputs may be any that keep to these rules, and one draw needn't show every extreme that they name: `col_blocks`: each row group names 2 different column blocks. Each row of slot_map takes every value once; slot t is held by index t // 2 of bas. `pair_list`: the first pair_count entries of a list are different block pairs, the rest are unused; of the pairs whose slots one index of bas holds, a list names at most 1 among its used entries, and in every draw some index of bas is named 1 times by every list of a row group. `pair_count`: in every row group some slab's list uses all 32 entries.
All inputs are finite; a program needn't handle non-finite values.
Results may differ from a plain program's by a relative error of at most 0.02.
Values may be sent and summed in bfloat16 or wider, within the bound.
No kernel may reach another device: no remote copies, remote signals or barrier semaphores. Data moves between devices by JAX's collectives and lax.ppermute only.
A program may use at most 32 MiB of HBM per device.

v0:
```python
import jax
import jax.numpy as jnp
from jax import lax
from jax.sharding import PartitionSpec as P

BLK = 128
NCB = 2


def on_device(three_centre, occ_coeff, amp_coeff, col_blocks, slot_map, pair_list, pair_count):
    aux_local, rows_local, width = three_centre.shape
    row_blocks = rows_local // BLK
    integrals = three_centre.reshape(aux_local * rows_local, width)
    columns = col_blocks[0]
    stacked = jnp.stack((occ_coeff, amp_coeff), 0)
    piece = lax.all_gather(stacked, "orb", axis=1, tiled=True)
    chosen = jnp.concatenate(
        [lax.dynamic_slice_in_dim(piece, columns[k] * BLK, BLK, 2) for k in range(NCB)], 2
    )
    halves = jnp.einsum(
        "cil,zl->ciz", chosen, integrals, preferred_element_type=jnp.float32
    ).astype(jnp.bfloat16)
    occ_total = halves.shape[1]
    occ_half = halves[0].reshape(occ_total * aux_local, rows_local)
    amp_half = halves[1].reshape(occ_total * aux_local, rows_local)
    product = lax.dot_general(
        occ_half, amp_half, (((0,), (0,)), ((), ())), preferred_element_type=jnp.float32
    )
    pair_total = row_blocks * row_blocks
    blocks = (
        product.reshape(row_blocks, BLK, row_blocks, BLK)
        .transpose(0, 2, 1, 3)
        .reshape(pair_total, BLK, BLK)
    )
    tasks = pair_list[0, 0]
    valid = jnp.arange(tasks.shape[0], dtype=jnp.int32) < pair_count[0, 0]
    slot_order = slot_map[0]
    listed = jnp.zeros((pair_total,), jnp.float32).at[tasks].max(valid.astype(jnp.float32))
    partial_value = (
        jnp.zeros((pair_total, BLK, BLK), jnp.float32)
        .at[slot_order]
        .set(blocks * listed[:, None, None])
    )
    owned = lax.psum_scatter(
        partial_value.astype(jnp.bfloat16), "bas", scatter_dimension=0, tiled=True
    ).astype(jnp.float32)
    return owned[None]


def solution(mesh):
    placed = (
        P("bas", "orb", None),
        P("orb", None),
        P("orb", None),
        P("orb", None),
        P("orb", None),
        P("orb", "bas", None),
        P("orb", "bas"),
    )
    return jax.shard_map(
        on_device,
        mesh=mesh,
        in_specs=placed,
        out_specs=P("orb", "bas", None, None),
        check_vma=False,
    )
```

profile of v0, /device:TPU:1, one launch (start us, length us, event | category | flops | bytes accessed | tf_op | source)
XLA Modules:
  0.0 284.6 jit_solution(18320501092767892007)
XLA Ops:
  6.5 0.0 copy-start
  6.5 0.0 all-gather.2.cloned.1.call-start
  6.5 1.5 pad_maximum_fusion
  8.0 0.0 all-gather.2.cloned.1.call-update
  8.1 0.0 reduce-scatter.2.cloned.1.call-start
  8.1 1.3 fusion.9
  11.4 0.7 fusion.4
  12.0 0.8 scatter_custom_fusion
  12.8 0.7 fusion.3
  13.4 100.1 %all-gather.2.cloned.1.call-done = bf16[2,512,1024]{2,1,0:T(8,128)(2,1)} async-done(((bf16[2,16,1024]{2,1,0:T(8,128)(2,1)}), bf16[2,512,1024]{2,1,0:T(8,128)(2,1)}) %all-gather.2.cloned.1.call-update) | async-done | bytes 2097168 | tf_op jit(solution)/shard_map/all_gather | solution.py:16
  113.5 1.1 constant_dynamic-slice_fusion.1
  114.6 0.0 copy-done
  114.6 1.3 convolution_convert_fusion
  115.9 2.5 fusion.8
  118.4 2.7 reshape_squeeze.7
  121.1 2.6 copy.9
  123.7 2.7 reshape_squeeze.6
  126.3 2.6 copy.8
  128.9 4.6 %fusion.10 = f32[8,128,8,128]{3,1,2,0:T(8,128)S(1)} fusion(bf16[8,128,1024,1]{2,1,3,0:T(8,128)(2,1)} %bitcast.42, bf16[8,128,1024,1]{2,1,0,3:T(8,128)(2,1)} %bitcast.41), kind=kOutput, calls=%fused_computation.21 | convolution fusion | flops 2147483648 | bytes 8388608 | tf_op jit(solution)/shard_map/dot_general | solution.py:26
  133.5 2.3 bitcast_multiply_fusion
  135.8 2.4 broadcast_in_dim.15
  138.3 12.1 %scatter_fusion = f32[64,128,128]{2,1,0:T(8,128)} fusion(f32[64,128,128]{2,1,0:T(8,128)} %broadcast_in_dim.15, s32[64]{0:T(128)S(1)} %fusion.3, f32[64,128,128]{2,1,0:T(8,128)} %bitcast_multiply_fusion), kind=kCustom, calls=%fused_computation.1 | custom fusion | bytes 12583168 | tf_op jit(solution)/shard_map/scatter | solution.py:42
  150.4 3.9 %convert_element_type.12 = bf16[64,128,128]{2,1,0:T(8,128)(2,1)} convert(f32[64,128,128]{2,1,0:T(8,128)} %scatter_fusion) | non-fusion elementwise | flops 1048576 | bytes 6291456 | tf_op jit(solution)/shard_map/convert_element_type | solution.py:45
  154.3 0.0 reduce-scatter.2.cloned.1.call-update
  154.3 121.9 %reduce-scatter.2.cloned.1.call-done = bf16[2,128,128]{2,1,0:T(8,128)(2,1)} async-done(((bf16[64,128,128]{2,1,0:T(8,128)(2,1)}), bf16[2,128,128]{2,1,0:T(8,128)(2,1)}) %reduce-scatter.2.cloned.1.call-update) | async-done | bytes 65552 | tf_op jit(solution)/shard_map/reduce_scatter | solution.py:44
  276.2 1.5 bitcast_convert_fusion
  (1 shorter events, 0.0 us)
Async XLA Ops:
  6.5 108.1 %copy-start = (bf16[2,1024,256]{2,1,0:T(8,128)(2,1)S(1)}, bf16[2,1024,256]{2,1,0:T(8,128)(2,1)}, u32[]{:S(2)}) copy-start(bf16[2,1024,256]{2,1,0:T(8,128)(2,1)} %param.7) | copy-start | bytes 3145732
  6.5 107.0 %all-gather.2.cloned.1.call-start = ((), (), s32[]{:S(2)}) async-start(), calls=%async_computation.1 | async-start | bytes 2162688 | tf_op jit(solution)/shard_map/all_gather | solution.py:16
  8.1 268.2 %reduce-scatter.2.cloned.1.call-start = ((), (), s32[]{:S(2)}) async-start(), calls=%async_computation.2 | async-start | bytes 2162688 | tf_op jit(solution)/shard_map/reduce_scatter | solution.py:44
Sparse Core Ops, SparseCore 0:
  11.7 101.7 all-gather.1
  154.4 121.7 reduce-scatter.1
where the time goes:
time: 288 us; the launch traced here: 285 us
  waiting for transfers between devices  222 us (77%)
  local copies, waits for them, and re-layouts  30 us (10%)
  between operations  15.4 us (5%)
  other arithmetic  11.3 us (4%)
  matrix products  5.88 us (2%)
    reduce_scatter x1, waiting for transfers between devices, on_device(): lax.psum_scatter(partial_value.astype(jnp.bfloat16), 'bas', scatter_dimen...  122 us
    all_gather x1, waiting for transfers between devices, on_device(): piece = lax.all_gather(stacked, 'orb', axis=1, tiled=True)  100 us
    scatter x1, local copies, waits for them, and re-layouts, on_device(): partial_value = jnp.zeros((pair_total, BLK, BLK), jnp.float32).at[slot_or...  12.1 us
  transfers between devices with their start and end apart: 2, of which 2 were waited for; matrix products, arithmetic and copies ran while one was open for 1% of the time, Pallas kernels for 0%

commit v1 on v0

v1 whole, which is shorter than its diff:
```python
import jax
import jax.numpy as jnp
from jax import lax
from jax.experimental import pallas as pl
from jax.experimental.pallas import tpu as pltpu
from jax.sharding import Mesh, PartitionSpec as P

BLK = 128
NCB = 2
ORB = ("x", "yh")
BAS = ("yl", "z", "c")
TAG = 8
F32 = jnp.float32
BF16 = jnp.bfloat16


def contract(a, b, da, db):
    return lax.dot_general(a, b, (((da,), (db,)), ((), ())), preferred_element_type=F32)


def exchange_kernel(pairs, count, slots, own, other, g_ref, out, blocks, place, tag):
    owners = out.shape[0]
    aux, rows, _ = g_ref.shape
    row_blocks = rows // BLK

    def clear(d, _):
        place[d] = 0
        tag[d] = 2
        return 0

    lax.fori_loop(0, owners, clear, 0, unroll=True)

    def enter(e, _):
        p = pairs[0, 0, e]
        slot = slots[0, p]
        d = slot // 2
        place[d] = p
        tag[d] = slot - 2 * d
        return 0

    lax.fori_loop(0, count[0, 0], enter, 0)

    def wide(ref, t):
        return jnp.concatenate([ref[t, k] for k in range(NCB)], axis=1)

    s = contract(wide(own, 0), wide(own, 1), 0, 0) + contract(wide(other, 0), wide(other, 1), 0, 0)
    s = s.astype(BF16)
    g = jnp.concatenate([g_ref[q] for q in range(aux)], axis=1)
    step = 2 * BLK
    for m in range(rows // step):
        t = jnp.concatenate(
            [contract(g_ref[q, m * step:(m + 1) * step], s, 1, 0).astype(BF16) for q in range(aux)], axis=1
        )
        full = contract(t, g, 1, 1).astype(BF16)
        for h in range(2):
            for n in range(row_blocks):
                blocks[(2 * m + h) * row_blocks + n] = full[h * BLK:(h + 1) * BLK, n * BLK:(n + 1) * BLK]

    def send(d, _):
        out[d, 0:BLK] = blocks[place[d]]
        out[d, BLK:BLK + TAG] = jnp.full((TAG, BLK), tag[d], jnp.int32).astype(F32).astype(BF16)
        return 0

    lax.fori_loop(0, owners, send, 0, unroll=4)


def sum_kernel(got, out):
    def add(d, total):
        mark = got[d, BLK:BLK + TAG].astype(F32)
        piece = got[d, 0:BLK].astype(F32).reshape(BLK // TAG, TAG, BLK)
        return tuple(
            total[k] + jnp.where((mark == k)[None], piece, 0.0) for k in range(2)
        )

    zero = jnp.zeros((BLK // TAG, TAG, BLK), F32)
    total = lax.fori_loop(0, got.shape[0], add, (zero, zero))
    for k in range(2):
        out[0, k] = total[k].reshape(BLK, BLK)


def on_device(three_centre, occ_coeff, amp_coeff, col_blocks, slot_map, pair_list, pair_count):
    n_orb = lax.axis_size(ORB)
    n_bas = lax.axis_size(BAS)
    own_rows, width = occ_coeff.shape
    half = own_rows // 2
    col_total = width // BLK
    core = lax.axis_index("c")

    def cut(coeff):
        part = lax.dynamic_slice_in_dim(coeff, core * half, half, 0)
        return part.reshape(half, col_total, BLK).transpose(1, 0, 2)

    mine = jnp.concatenate([cut(occ_coeff), cut(amp_coeff)], 0)
    mine = jnp.broadcast_to(mine.reshape(1, 2 * col_total * half, BLK), (n_orb, 2 * col_total * half, BLK))
    got = lax.all_to_all(mine, ORB, 0, 0, tiled=True)
    got = got.reshape(n_orb, 2, col_total, half, BLK)
    own = jnp.stack(
        [lax.dynamic_index_in_dim(got, col_blocks[0, k], 2, keepdims=False) for k in range(NCB)], 0
    )
    own = own.transpose(2, 0, 1, 3, 4).reshape(2, NCB, n_orb * half, BLK)
    other = lax.ppermute(own, "c", [(0, 1), (1, 0)])

    vmem = pl.BlockSpec(memory_space=pltpu.VMEM)
    smem = pl.BlockSpec(memory_space=pltpu.SMEM)
    row_blocks = three_centre.shape[1] // BLK
    send = pl.pallas_call(
        exchange_kernel,
        out_shape=jax.ShapeDtypeStruct((n_bas, BLK + TAG, BLK), BF16),
        in_specs=[smem, smem, smem, vmem, vmem, vmem],
        out_specs=vmem,
        scratch_shapes=[
            pltpu.VMEM((row_blocks * row_blocks, BLK, BLK), BF16),
            pltpu.SMEM((n_bas,), jnp.int32),
            pltpu.SMEM((n_bas,), jnp.int32),
        ],
        compiler_params=pltpu.CompilerParams(vmem_limit_bytes=40 * 1024 * 1024),
        name="exchange_blocks",
    )(pair_list, pair_count, slot_map, own, other, three_centre)
    arrived = lax.all_to_all(send, BAS, 0, 0, tiled=True)
    return pl.pallas_call(
        sum_kernel,
        out_shape=jax.ShapeDtypeStruct((1, 2, BLK, BLK), F32),
        in_specs=[vmem],
        out_specs=vmem,
        compiler_params=pltpu.CompilerParams(vmem_limit_bytes=40 * 1024 * 1024),
        name="sum_slots",
    )(arrived)


def solution(mesh):
    fine = Mesh(mesh.devices.reshape(8, 4, 2, 8, 2), ("x", "yh", "yl", "z", "c"))
    placed = (
        P(BAS, ORB, None),
        P(ORB, None),
        P(ORB, None),
        P(ORB, None),
        P(ORB, None),
        P(ORB, BAS, None),
        P(ORB, BAS),
    )
    return jax.shard_map(
        on_device,
        mesh=fine,
        in_specs=placed,
        out_specs=P(ORB, BAS, None, None),
        check_vma=False,
    )
```

time: 288 us -> 101 us (0.35); the launches traced: 285 us -> 101 us
  waiting for transfers between devices: 222 us -> 19.8 us
  blocking collectives: 0 us -> 47.7 us
  local copies, waits for them, and re-layouts: 30 us -> 2.63 us
  starting transfers between devices: 0.04 us -> 22.1 us
  other arithmetic: 11.3 us -> 0.05 us
  between operations: 15.4 us -> 4.46 us
  matrix products: 5.88 us -> 0 us
  Pallas kernels: 0 us -> 4.32 us
    reduce_scatter x1 -> x0, waiting for transfers between devices: 122 us -> none  [on_device(): lax.psum_scatter(partial_value.astype(jnp.bfloat16), 'bas', scatter_dimen...]
    all_gather x1 -> x0, waiting for transfers between devices: 100 us -> none  [on_device(): piece = lax.all_gather(stacked, 'orb', axis=1, tiled=True)]
    all_to_all x0 -> x1, blocking collectives: none -> 47.7 us  [on_device(): arrived = lax.all_to_all(send, BAS, 0, 0, tiled=True)]
    all_to_all x0 -> x1, waiting for transfers between devices: none -> 19.3 us  [on_device(): got = lax.all_to_all(mine, ORB, 0, 0, tiled=True)]
    all_to_all x0 -> x1, starting transfers between devices: none -> 13.6 us  [on_device(): got = lax.all_to_all(mine, ORB, 0, 0, tiled=True)]
    scatter x1 -> x0, local copies, waits for them, and re-layouts: 12.1 us -> none  [on_device(): partial_value = jnp.zeros((pair_total, BLK, BLK), jnp.float32).at[slot_or...]
    ppermute x0 -> x1, starting transfers between devices: none -> 8.51 us  [on_device(): other = lax.ppermute(own, 'c', [(0, 1), (1, 0)])]
    dot_general x2 -> x0, matrix products: 5.88 us -> none  [the longest x1 4.59 us: on_device(): lax.dot_general(occ_half, amp_half, (((0,), (0,)), ((), ())), preferred_e...]
where the time goes in v1:
time: 101 us
  blocking collectives  47.7 us (47%)
  starting transfers between devices  22.1 us (22%)
  waiting for transfers between devices  19.8 us (20%)
  between operations  4.46 us (4%)
  Pallas kernels  4.32 us (4%)
  local copies, waits for them, and re-layouts  2.63 us (3%)
    all_to_all x1, blocking collectives, on_device(): arrived = lax.all_to_all(send, BAS, 0, 0, tiled=True)  47.7 us
    all_to_all x1, waiting for transfers between devices, on_device(): got = lax.all_to_all(mine, ORB, 0, 0, tiled=True)  19.3 us
    all_to_all x1, starting transfers between devices, on_device(): got = lax.all_to_all(mine, ORB, 0, 0, tiled=True)  13.6 us
    ppermute x1, starting transfers between devices, on_device(): other = lax.ppermute(own, 'c', [(0, 1), (1, 0)])  8.51 us
    pallas_call x1, Pallas kernels, on_device(): pl.pallas_call(exchange_kernel, out_shape=jax.ShapeDtypeStruct((n_bas, BL...  2.89 us
  transfers between devices with their start and end apart: 2, of which 2 were waited for; matrix products, arithmetic and copies ran while one was open for 1% of the time, Pallas kernels for 0%

profile of v1, /device:TPU:1, one launch (start us, length us, event | category | flops | bytes accessed | tf_op | source)
XLA Modules:
  0.0 101.0 jit_solution(10078621076906602034)
XLA Ops:
  0.0 0.7 dynamic-slice_bitcast_fusion.2
  0.7 1.2 %broadcast_in_dim.8 = bf16[32,128,128]{2,1,0:T(8,128)(2,1)} broadcast(bf16[128,128]{1,0:T(8,128)(2,1)S(1)} %maximum_bitcast_fusion.1), dimensions={1,2} | broadcast | bytes 1081344 | tf_op jit(solution)/shard_map/broadcast_in_dim | solution.py:94
  1.9 0.0 copy-start.3
  1.9 0.0 copy-start
  2.0 0.0 copy-start.1
  2.0 0.0 copy-start.2
  2.0 13.6 %all-to-all-start = ((bf16[32,128,128]{2,1,0:T(8,128)(2,1)}), bf16[32,128,128]{2,1,0:T(8,128)(2,1)S(1)}, u32[]{:S(2)}, u32[]{:S(2)}) async-start(bf16[32,128,128]{2,1,0:T(8,128)(2,1)} %broadcast_in_dim.8), calls=%async_computation | async-start | bytes 2097152 | tf_op jit(solution)/shard_map/all_to_all | solution.py:95
  15.5 0.0 copy-done.3
  15.5 0.6 fusion
  19.9 19.3 %all-to-all-done = bf16[32,128,128]{2,1,0:T(8,128)(2,1)S(1)} async-done(((bf16[32,128,128]{2,1,0:T(8,128)(2,1)}), bf16[32,128,128]{2,1,0:T(8,128)(2,1)S(1)}, u32[]{:S(2)}, u32[]{:S(2)}) %all-to-all-start) | async-done | bytes 1048608 | tf_op jit(solution)/shard_map/all_to_all | solution.py:95
  39.2 0.1 dynamic-slice_bitcast_fusion.1
  39.3 8.5 %collective-permute-start = (bf16[2,2,256,128]{3,2,1,0:T(8,128)(2,1)S(1)}, bf16[2,2,256,128]{3,2,1,0:T(8,128)(2,1)S(1)}, u32[]{:S(2)}, u32[]{:S(2)}) collective-permute-start(bf16[2,2,256,128]{3,2,1,0:T(8,128)(2,1)S(1)} %copy_bitcast_fusion.own), channel_id=1, source_target_pairs={{0,1},{1,0},{2,3},{3,2},{4,5},{5,4},{6,7},{7,6},{8,9},{9,8},{10,11... | collective-permute-start | bytes 786440 | tf_op jit(solution)/shard_map/ppermute | solution.py:101
  48.5 0.5 collective-permute-done.other
  49.0 0.0 copy-done
  49.0 0.0 copy-done.1
  49.0 0.0 copy-done.2
  49.0 2.9 %exchange_blocks.1 = bf16[32,136,128]{2,1,0:T(8,128)(2,1)S(1)} custom-call(s32[1,1,32]{2,1,0:T(1,128)S(1)} %copy-done.1, s32[1,1]{1,0:T(1,128)S(6)} %copy.10.count, s32[1,64]{1,0:T(1,128)S(1)} %copy-done.2, bf16[2,2,256,128]{3,2,1,0:T(8,128)(2,1)S(1)} %copy_bitcast_fusion.own, bf16[2,2,256,128]{3,2,1,0:T(8,128)(2,1)S(1)} %collective-permute-done.other, ...), custom_call_target="tpu_custom_call" | custom-call | tf_op jit(solution)/shard_map/exchange_blocks/pallas_call | solution.py:106
  51.9 47.7 %all_to_all.10.got = bf16[32,136,128]{2,1,0:T(8,128)(2,1)S(1)} all-to-all(bf16[32,136,128]{2,1,0:T(8,128)(2,1)S(1)} %exchange_blocks.1), channel_id=1, replica_groups=mesh['x'=8,'yh'=4,'yl'=2,'z'=8,'c'=2] {'yl','z','c'}, dimensions={0} | all-to-all | bytes 2228224 | tf_op jit(solution)/shard_map/all_to_all | solution.py:119
  99.5 1.4 %sum_slots.1 = f32[1,2,128,128]{3,2,1,0:T(8,128)} custom-call(bf16[32,136,128]{2,1,0:T(8,128)(2,1)S(1)} %all_to_all.10.got), custom_call_target="tpu_custom_call" | custom-call | tf_op jit(solution)/shard_map/sum_slots/pallas_call | solution.py:120
  (2 shorter events, 0.1 us)
Async XLA Ops:
  1.9 13.6 %copy-start.3 = (s32[1,2]{1,0:T(1,128)S(1)}, s32[1,2]{1,0:T(1,128)}, u32[]{:S(2)}) copy-start(s32[1,2]{1,0:T(1,128)} %param.10) | copy-start | bytes 28
  1.9 47.0 %copy-start = (bf16[2,1024,256]{2,1,0:T(8,128)(2,1)S(1)}, bf16[2,1024,256]{2,1,0:T(8,128)(2,1)}, u32[]{:S(2)}) copy-start(bf16[2,1024,256]{2,1,0:T(8,128)(2,1)} %g_ref.1) | copy-start | bytes 3145732
  2.0 47.0 %copy-start.1 = (s32[1,1,32]{2,1,0:T(1,128)S(1)}, s32[1,1,32]{2,1,0:T(1,128)}, u32[]{:S(2)}) copy-start(s32[1,1,32]{2,1,0:T(1,128)} %pairs.1) | copy-start | bytes 388
  2.0 47.0 %copy-start.2 = (s32[1,64]{1,0:T(1,128)S(1)}, s32[1,64]{1,0:T(1,128)}, u32[]{:S(2)}) copy-start(s32[1,64]{1,0:T(1,128)} %slots.1) | copy-start | bytes 772
  2.0 37.2 %all-to-all-start = ((bf16[32,128,128]{2,1,0:T(8,128)(2,1)}), bf16[32,128,128]{2,1,0:T(8,128)(2,1)S(1)}, u32[]{:S(2)}, u32[]{:S(2)}) async-start(bf16[32,128,128]{2,1,0:T(8,128)(2,1)} %broadcast_in_dim.8), calls=%async_computation | async-start | bytes 2097152 | tf_op jit(solution)/shard_map/all_to_all | solution.py:95
  39.3 9.7 %collective-permute-start = (bf16[2,2,256,128]{3,2,1,0:T(8,128)(2,1)S(1)}, bf16[2,2,256,128]{3,2,1,0:T(8,128)(2,1)S(1)}, u32[]{:S(2)}, u32[]{:S(2)}) collective-permute-start(bf16[2,2,256,128]{3,2,1,0:T(8,128)(2,1)S(1)} %copy_bitcast_fusion.own), channel_id=1, source_target_pairs={{0,1},{1,0},{2,3},{3,2},{4,5},{5,4},{6,7},{7,6},{8,9},{9,8},{10,11... | collective-permute-start | bytes 786440 | tf_op jit(solution)/shard_map/ppermute | solution.py:101

commit v2 on v1

--- a/solution.py
+++ b/solution.py
@@ -18,7 +18,7 @@
     return lax.dot_general(a, b, (((da,), (db,)), ((), ())), preferred_element_type=F32)
 
 
-def exchange_kernel(pairs, count, slots, own, other, g_ref, out, blocks, place, tag):
+def exchange_kernel(pairs, count, slots, near, far, g_ref, out, blocks, place, tag):
     owners = out.shape[0]
     aux, rows, _ = g_ref.shape
     row_blocks = rows // BLK
@@ -40,10 +40,14 @@
 
     lax.fori_loop(0, count[0, 0], enter, 0)
 
-    def wide(ref, t):
-        return jnp.concatenate([ref[t, k] for k in range(NCB)], axis=1)
+    def wide(t):
+        return jnp.concatenate(
+            [jnp.concatenate([ref[t, k] for k in range(NCB)], axis=1) for ref in (near, far)], axis=0
+        )
 
-    s = contract(wide(own, 0), wide(own, 1), 0, 0) + contract(wide(other, 0), wide(other, 1), 0, 0)
+    first, second = wide(0), wide(1)
+    is_occ = lax.axis_index("yl") == 0
+    s = contract(jnp.where(is_occ, first, second), jnp.where(is_occ, second, first), 0, 0)
     s = s.astype(BF16)
     g = jnp.concatenate([g_ref[q] for q in range(aux)], axis=1)
     step = 2 * BLK
@@ -84,21 +88,24 @@
     own_rows, width = occ_coeff.shape
     half = own_rows // 2
     col_total = width // BLK
-    core = lax.axis_index("c")
+    swap = [(0, 1), (1, 0)]
 
-    def cut(coeff):
-        part = lax.dynamic_slice_in_dim(coeff, core * half, half, 0)
-        return part.reshape(half, col_total, BLK).transpose(1, 0, 2)
-
-    mine = jnp.concatenate([cut(occ_coeff), cut(amp_coeff)], 0)
-    mine = jnp.broadcast_to(mine.reshape(1, 2 * col_total * half, BLK), (n_orb, 2 * col_total * half, BLK))
-    got = lax.all_to_all(mine, ORB, 0, 0, tiled=True)
-    got = got.reshape(n_orb, 2, col_total, half, BLK)
+    tensor = jnp.where(lax.axis_index("yl") == 0, occ_coeff, amp_coeff)
+    mine = lax.dynamic_slice_in_dim(tensor, lax.axis_index("c") * half, half, 0)
+    mine = mine.reshape(half, col_total, BLK).transpose(1, 0, 2).reshape(1, col_total * half, BLK)
+    mine = jnp.broadcast_to(mine, (n_orb, col_total * half, BLK))
+    got = lax.all_to_all(mine, ORB, 0, 0, tiled=True).reshape(n_orb, col_total, half, BLK)
     own = jnp.stack(
-        [lax.dynamic_index_in_dim(got, col_blocks[0, k], 2, keepdims=False) for k in range(NCB)], 0
+        [
+            lax.dynamic_index_in_dim(got, col_blocks[0, k], 1, keepdims=False).reshape(n_orb * half, BLK)
+            for k in range(NCB)
+        ],
+        0,
     )
-    own = own.transpose(2, 0, 1, 3, 4).reshape(2, NCB, n_orb * half, BLK)
-    other = lax.ppermute(own, "c", [(0, 1), (1, 0)])
+    other = lax.ppermute(own, "yl", swap)
+    near = jnp.stack((own, other), 0)
+    far = lax.ppermute(near, "c", swap)
+    coeffs = (near, far)
 
     vmem = pl.BlockSpec(memory_space=pltpu.VMEM)
     smem = pl.BlockSpec(memory_space=pltpu.SMEM)
@@ -106,7 +113,7 @@
     send = pl.pallas_call(
         exchange_kernel,
         out_shape=jax.ShapeDtypeStruct((n_bas, BLK + TAG, BLK), BF16),
-        in_specs=[smem, smem, smem, vmem, vmem, vmem],
+        in_specs=[smem, smem, smem] + [vmem] * (len(coeffs) + 1),
         out_specs=vmem,
         scratch_shapes=[
             pltpu.VMEM((row_blocks * row_blocks, BLK, BLK), BF16),
@@ -115,7 +122,7 @@
         ],
         compiler_params=pltpu.CompilerParams(vmem_limit_bytes=40 * 1024 * 1024),
         name="exchange_blocks",
-    )(pair_list, pair_count, slot_map, own, other, three_centre)
+    )(pair_list, pair_count, slot_map, *coeffs, three_centre)
     arrived = lax.all_to_all(send, BAS, 0, 0, tiled=True)
     return pl.pallas_call(
         sum_kernel,

time: 101 us -> 97.6 us (0.966)
  waiting for transfers between devices: 19.8 us -> 12.5 us
  starting transfers between devices: 22.1 us -> 26.3 us
  local copies, waits for them, and re-layouts: 2.63 us -> 1.55 us
    all_to_all x1, waiting for transfers between devices: 19.3 us -> 9.68 us  [on_device(): lax.all_to_all(mine, ORB, 0, 0, tiled=True)]
    ppermute x1 -> x2, starting transfers between devices: 8.51 us -> 12.7 us  [the longest x1 7.15 us: on_device(): far = lax.ppermute(near, 'c', swap)]
    ppermute x1 -> x2, waiting for transfers between devices: 0.49 us -> 2.84 us  [the longest x1 2.34 us: on_device(): other = lax.ppermute(own, 'yl', swap)]
  transfers between devices with their start and end apart: 2 -> 3, of which waited for: 2 -> 3; matrix products, arithmetic and copies ran while one was open for 1% -> 1% of each run, Pallas kernels for 0% -> 0%
where the time goes in v2:
time: 97.6 us; the launch traced here: 96.9 us
  blocking collectives  47 us (48%)
  starting transfers between devices  26.3 us (27%)
  waiting for transfers between devices  12.5 us (13%)
  Pallas kernels  4.4 us (5%)
  between operations  4.38 us (4%)
  local copies, waits for them, and re-layouts  1.55 us (2%)
    all_to_all x1, blocking collectives, on_device(): arrived = lax.all_to_all(send, BAS, 0, 0, tiled=True)  47 us
    all_to_all x1, starting transfers between devices, on_device(): lax.all_to_all(mine, ORB, 0, 0, tiled=True)  13.5 us
    all_to_all x1, waiting for transfers between devices, on_device(): lax.all_to_all(mine, ORB, 0, 0, tiled=True)  9.68 us
    ppermute x1, starting transfers between devices, on_device(): far = lax.ppermute(near, 'c', swap)  7.15 us
    ppermute x1, starting transfers between devices, on_device(): other = lax.ppermute(own, 'yl', swap)  5.55 us
    pallas_call x1, Pallas kernels, on_device(): pl.pallas_call(exchange_kernel, out_shape=jax.ShapeDtypeStruct((n_bas, BL...  2.97 us
    ppermute x1, waiting for transfers between devices, on_device(): other = lax.ppermute(own, 'yl', swap)  2.34 us
  transfers between devices with their start and end apart: 3, of which 3 were waited for; matrix products, arithmetic and copies ran while one was open for 1% of the time, Pallas kernels for 0%

profile of v2, /device:TPU:1, one launch (start us, length us, event | category | flops | bytes accessed | tf_op | source)
XLA Modules:
  0.0 96.9 jit_solution(458643522469418021)
XLA Ops:
  0.0 0.0 copy-start.3
  0.0 0.8 fusion
  0.8 0.9 broadcast_in_dim.8
  1.7 0.0 copy-start
  1.7 0.0 copy-start.1
  1.7 0.0 copy-start.2
  1.7 13.5 %all-to-all-start = ((bf16[32,64,128]{2,1,0:T(8,128)(2,1)}), bf16[32,64,128]{2,1,0:T(8,128)(2,1)S(1)}, u32[]{:S(2)}, u32[]{:S(2)}) async-start(bf16[32,64,128]{2,1,0:T(8,128)(2,1)} %broadcast_in_dim.8), calls=%async_computation | async-start | bytes 1048576 | tf_op jit(solution)/shard_map/all_to_all | solution.py:97
  15.2 0.0 copy-done.3
  15.2 0.6 fusion.2
  19.5 9.7 %all-to-all-done = bf16[32,64,128]{2,1,0:T(8,128)(2,1)S(1)} async-done(((bf16[32,64,128]{2,1,0:T(8,128)(2,1)}), bf16[32,64,128]{2,1,0:T(8,128)(2,1)S(1)}, u32[]{:S(2)}, u32[]{:S(2)}) %all-to-all-start) | async-done | bytes 524320 | tf_op jit(solution)/shard_map/all_to_all | solution.py:97
  29.3 5.6 %collective-permute-start = (bf16[2,256,128]{2,1,0:T(8,128)(2,1)S(1)}, bf16[2,256,128]{2,1,0:T(8,128)(2,1)S(1)}, u32[]{:S(2)}, u32[]{:S(2)}) collective-permute-start(bf16[2,256,128]{2,1,0:T(8,128)(2,1)S(1)} %get-tuple-element.8), channel_id=1, source_target_pairs={{0,16},{16,0},{1,17},{17,1},{2,18},{18,2},{3,19},{19,3},{4,20},{20... | collective-permute-start | bytes 393224 | tf_op jit(solution)/shard_map/ppermute | solution.py:105
  34.8 2.3 %collective-permute-done = bf16[2,256,128]{2,1,0:T(8,128)(2,1)S(1)} collective-permute-done((bf16[2,256,128]{2,1,0:T(8,128)(2,1)S(1)}, bf16[2,256,128]{2,1,0:T(8,128)(2,1)S(1)}, u32[]{:S(2)}, u32[]{:S(2)}) %collective-permute-start) | collective-permute-done | bytes 131104 | tf_op jit(solution)/shard_map/ppermute | solution.py:105
  37.2 7.2 %collective-permute-start.1 = (bf16[2,2,256,128]{3,2,1,0:T(8,128)(2,1)S(1)}, bf16[2,2,256,128]{3,2,1,0:T(8,128)(2,1)S(1)}, u32[]{:S(2)}, u32[]{:S(2)}) collective-permute-start(bf16[2,2,256,128]{3,2,1,0:T(8,128)(2,1)S(1)} %pad_maximum_fusion.near), channel_id=1, source_target_pairs={{0,1},{1,0},{2,3},{3,2},{4,5},{5,4},{6,7},{7,6},{8,9},{9,8},{10,11... | collective-permute-start | bytes 786440 | tf_op jit(solution)/shard_map/ppermute | solution.py:107
  45.0 0.5 collective-permute-done.1.far
  45.5 0.0 copy-done
  45.5 0.0 copy-done.1
  45.5 0.0 copy-done.2
  45.5 3.0 %exchange_blocks.1 = bf16[32,136,128]{2,1,0:T(8,128)(2,1)S(1)} custom-call(s32[1,1,32]{2,1,0:T(1,128)S(1)} %copy-done.1, s32[1,1]{1,0:T(1,128)S(6)} %copy.8.count, s32[1,64]{1,0:T(1,128)S(1)} %copy-done.2, bf16[2,2,256,128]{3,2,1,0:T(8,128)(2,1)S(1)} %pad_maximum_fusion.near, bf16[2,2,256,128]{3,2,1,0:T(8,128)(2,1)S(1)} %collective-permute-done.1.far, ...), custom_call_target="tpu_custom_call" | custom-call | tf_op jit(solution)/shard_map/exchange_blocks/pallas_call | solution.py:113
  48.5 47.0 %all_to_all.10.got = bf16[32,136,128]{2,1,0:T(8,128)(2,1)S(1)} all-to-all(bf16[32,136,128]{2,1,0:T(8,128)(2,1)S(1)} %exchange_blocks.1), channel_id=1, replica_groups=mesh['x'=8,'yh'=4,'yl'=2,'z'=8,'c'=2] {'yl','z','c'}, dimensions={0} | all-to-all | bytes 2228224 | tf_op jit(solution)/shard_map/all_to_all | solution.py:126
  95.5 1.4 %sum_slots.1 = f32[1,2,128,128]{3,2,1,0:T(8,128)} custom-call(bf16[32,136,128]{2,1,0:T(8,128)(2,1)S(1)} %all_to_all.10.got), custom_call_target="tpu_custom_call" | custom-call | tf_op jit(solution)/shard_map/sum_slots/pallas_call | solution.py:127
  (3 shorter events, 0.1 us)
Async XLA Ops:
  0.0 15.2 %copy-start.3 = (s32[1,2]{1,0:T(1,128)S(1)}, s32[1,2]{1,0:T(1,128)}, u32[]{:S(2)}) copy-start(s32[1,2]{1,0:T(1,128)} %param.10) | copy-start | bytes 28
  1.7 43.8 %copy-start = (bf16[2,1024,256]{2,1,0:T(8,128)(2,1)S(1)}, bf16[2,1024,256]{2,1,0:T(8,128)(2,1)}, u32[]{:S(2)}) copy-start(bf16[2,1024,256]{2,1,0:T(8,128)(2,1)} %g_ref.1) | copy-start | bytes 3145732
  1.7 43.8 %copy-start.1 = (s32[1,1,32]{2,1,0:T(1,128)S(1)}, s32[1,1,32]{2,1,0:T(1,128)}, u32[]{:S(2)}) copy-start(s32[1,1,32]{2,1,0:T(1,128)} %pairs.1) | copy-start | bytes 388
  1.7 43.8 %copy-start.2 = (s32[1,64]{1,0:T(1,128)S(1)}, s32[1,64]{1,0:T(1,128)}, u32[]{:S(2)}) copy-start(s32[1,64]{1,0:T(1,128)} %slots.1) | copy-start | bytes 772
  1.7 27.5 %all-to-all-start = ((bf16[32,64,128]{2,1,0:T(8,128)(2,1)}), bf16[32,64,128]{2,1,0:T(8,128)(2,1)S(1)}, u32[]{:S(2)}, u32[]{:S(2)}) async-start(bf16[32,64,128]{2,1,0:T(8,128)(2,1)} %broadcast_in_dim.8), calls=%async_computation | async-start | bytes 1048576 | tf_op jit(solution)/shard_map/all_to_all | solution.py:97
  29.3 7.9 %collective-permute-start = (bf16[2,256,128]{2,1,0:T(8,128)(2,1)S(1)}, bf16[2,256,128]{2,1,0:T(8,128)(2,1)S(1)}, u32[]{:S(2)}, u32[]{:S(2)}) collective-permute-start(bf16[2,256,128]{2,1,0:T(8,128)(2,1)S(1)} %get-tuple-element.8), channel_id=1, source_target_pairs={{0,16},{16,0},{1,17},{17,1},{2,18},{18,2},{3,19},{19,3},{4,20},{20... | collective-permute-start | bytes 393224 | tf_op jit(solution)/shard_map/ppermute | solution.py:105
  37.2 8.3 %collective-permute-start.1 = (bf16[2,2,256,128]{3,2,1,0:T(8,128)(2,1)S(1)}, bf16[2,2,256,128]{3,2,1,0:T(8,128)(2,1)S(1)}, u32[]{:S(2)}, u32[]{:S(2)}) collective-permute-start(bf16[2,2,256,128]{3,2,1,0:T(8,128)(2,1)S(1)} %pad_maximum_fusion.near), channel_id=1, source_target_pairs={{0,1},{1,0},{2,3},{3,2},{4,5},{5,4},{6,7},{7,6},{8,9},{9,8},{10,11... | collective-permute-start | bytes 786440 | tf_op jit(solution)/shard_map/ppermute | solution.py:107

commit v3 on v2

v3 whole, which is shorter than its diff:
```python
import jax
import jax.numpy as jnp
from jax import lax
from jax.experimental import pallas as pl
from jax.experimental.pallas import tpu as pltpu
from jax.sharding import Mesh, PartitionSpec as P

BLK = 128
NCB = 2
OWN = 2
ORB = ("x", "yh")
FAR = ("yl", "zh")
BAS = ("yl", "zh", "zl", "c")
SWAP = ((0, 1), (1, 0))
F32 = jnp.float32
BF16 = jnp.bfloat16


def contract(a, b, da, db):
    return lax.dot_general(a, b, (((da,), (db,)), ((), ())), preferred_element_type=F32)


def exchange_kernel(*refs):
    listed, near, far, slabs, out, t_ref = refs[0:2], refs[2], refs[3], refs[4:8], refs[8], refs[9]
    owners = out.shape[0]
    aux, row_blocks, _, width = slabs[0].shape

    def wide(t):
        return jnp.concatenate(
            [jnp.concatenate([ref[t, k] for k in range(NCB)], axis=1) for ref in (near, far)], axis=0
        )

    first, second = wide(0), wide(1)
    is_occ = lax.axis_index("yl") == 0
    s = contract(jnp.where(is_occ, first, second), jnp.where(is_occ, second, first), 0, 0)
    s = s.astype(BF16)
    for k, g_ref in enumerate(slabs):
        for q in range(aux):
            for m in range(0, row_blocks, 2):
                t = contract(g_ref[q, m:m + 2].reshape(2 * BLK, width), s, 1, 0).astype(BF16)
                t_ref[k, q, m:m + 2] = t.reshape(2, BLK, width)

    quarter = lax.axis_index("zl") * 2 + lax.axis_index("c")

    def owner(j, _):
        slot = (j * 4 + quarter) * OWN
        total = [jnp.zeros((BLK, BLK), F32)] * OWN
        for k, g_ref in enumerate(slabs):
            pair = [listed[k // 2][k % 2, slot + h] for h in range(OWN)]
            p = jnp.maximum(jnp.maximum(pair[0], pair[1]), 0)
            row, col = p // row_blocks, p % row_blocks
            block = contract(t_ref[k, 0, row], g_ref[0, col], 1, 1)
            for q in range(1, aux):
                block = block + contract(t_ref[k, q, row], g_ref[q, col], 1, 1)
            total = [total[h] + jnp.where(pair[h] >= 0, block, 0.0) for h in range(OWN)]
        for h in range(OWN):
            out[j, h * BLK:(h + 1) * BLK] = total[h].astype(BF16)
        return 0

    lax.fori_loop(0, owners, owner, 0, unroll=2)


def select_kernel(columns, got, out):
    for k in range(NCB):
        out[k] = got[:, columns[0, k]]


def sum_kernel(got, out):
    for h in range(OWN):
        total = got[0, h * BLK:(h + 1) * BLK].astype(F32)
        for j in range(1, got.shape[0]):
            total = total + got[j, h * BLK:(h + 1) * BLK].astype(F32)
        out[0, h] = total


def listed_pairs(slot_map, pair_list, pair_count):
    slot = slot_map[0]
    ids = jnp.arange(slot.shape[0], dtype=jnp.int32)
    entry = pair_list[0, 0]
    used = jnp.arange(entry.shape[0], dtype=jnp.int32) < pair_count[0, 0]
    named = jnp.max(jnp.where(used[:, None] & (entry[:, None] == ids[None]), 1, 0), 0)
    at = (slot[:, None] == ids[None]) & (named[:, None] > 0)
    return jnp.max(jnp.where(at, ids[:, None], -1), 0)[None]


def on_device(three_centre, occ_coeff, amp_coeff, col_blocks, slot_map, pair_list, pair_count):
    n_orb = lax.axis_size(ORB)
    n_far = lax.axis_size(FAR)
    own_rows, width = occ_coeff.shape
    half = own_rows // 2
    col_total = width // BLK

    tensor = jnp.where(lax.axis_index("yl") == 0, occ_coeff, amp_coeff)
    mine = lax.dynamic_slice_in_dim(tensor, lax.axis_index("c") * half, half, 0)
    mine = mine.reshape(half, col_total, BLK).transpose(1, 0, 2).reshape(1, col_total * half, BLK)
    mine = jnp.broadcast_to(mine, (n_orb, col_total * half, BLK))
    got = lax.all_to_all(mine, ORB, 0, 0, tiled=True).reshape(n_orb, col_total, half, BLK)

    aux, rows, sel = three_centre.shape
    g = three_centre.reshape(aux, rows // BLK, BLK, sel)
    g_side = lax.ppermute(g, "zl", SWAP)
    g_core = lax.ppermute(g, "c", SWAP)
    listed = listed_pairs(slot_map, pair_list, pair_count)
    listed = jnp.concatenate((listed, lax.ppermute(listed, "zl", SWAP)), 0)
    listed_core = lax.ppermute(listed, "c", SWAP)
    got, listed_core = lax.optimization_barrier((got, listed_core))

    vmem = pl.BlockSpec(memory_space=pltpu.VMEM)
    smem = pl.BlockSpec(memory_space=pltpu.SMEM)
    own = pl.pallas_call(
        select_kernel,
        out_shape=jax.ShapeDtypeStruct((NCB, n_orb, half, BLK), BF16),
        in_specs=[smem, vmem],
        out_specs=vmem,
        name="select_columns",
    )(col_blocks, got).reshape(NCB, n_orb * half, BLK)
    g_side, own = lax.optimization_barrier((g_side, own))
    g_both = lax.ppermute(g_side, "c", SWAP)
    near = jnp.stack((own, lax.ppermute(own, "yl", SWAP)), 0)
    far = lax.ppermute(near, "c", SWAP)
    slabs = (g, g_side, g_core, g_both)

    send = pl.pallas_call(
        exchange_kernel,
        out_shape=jax.ShapeDtypeStruct((n_far, OWN * BLK, BLK), BF16),
        in_specs=[smem] * 2 + [vmem] * (2 + len(slabs)),
        out_specs=vmem,
        scratch_shapes=[pltpu.VMEM((len(slabs), aux, rows // BLK, BLK, sel), BF16)],
        compiler_params=pltpu.CompilerParams(vmem_limit_bytes=40 * 1024 * 1024),
        name="exchange_blocks",
    )(listed, listed_core, near, far, *slabs)
    arrived = lax.all_to_all(send, FAR, 0, 0, tiled=True)
    return pl.pallas_call(
        sum_kernel,
        out_shape=jax.ShapeDtypeStruct((1, OWN, BLK, BLK), F32),
        in_specs=[vmem],
        out_specs=vmem,
        compiler_params=pltpu.CompilerParams(vmem_limit_bytes=40 * 1024 * 1024),
        name="sum_slots",
    )(arrived)


def solution(mesh):
    fine = Mesh(mesh.devices.reshape(8, 4, 2, 4, 2, 2), ("x", "yh", "yl", "zh", "zl", "c"))
    placed = (
        P(BAS, ORB, None),
        P(ORB, None),
        P(ORB, None),
        P(ORB, None),
        P(ORB, None),
        P(ORB, BAS, None),
        P(ORB, BAS),
    )
    return jax.shard_map(
        on_device,
        mesh=fine,
        in_specs=placed,
        out_specs=P(ORB, BAS, None, None),
        check_vma=False,
    )
```

time: 97.6 us -> 92.1 us (0.944); the launches traced: 96.9 us -> 90.3 us
  blocking collectives: 47 us -> 29.9 us
  starting transfers between devices: 26.3 us -> 39.3 us
  between operations: 4.38 us -> 0.79 us
  waiting for transfers between devices: 12.5 us -> 9.7 us
  Pallas kernels: 4.4 us -> 6.44 us
  other arithmetic: 0.8 us -> 1.89 us
    all_to_all x1, blocking collectives: 47 us -> 29.9 us  [on_device(): arrived = lax.all_to_all(send, FAR, 0, 0, tiled=True)]
    ppermute x2 -> x7, starting transfers between devices: 12.7 us -> 26.6 us  [the longest x1 5.95 us: on_device(): listed_core = lax.ppermute(listed, 'c', SWAP)]
    all_to_all x1, waiting for transfers between devices: 9.68 us -> 0.94 us  [on_device(): lax.all_to_all(mine, ORB, 0, 0, tiled=True)]
    ppermute x2 -> x7, waiting for transfers between devices: 2.84 us -> 8.76 us  [the longest x1 4.79 us: on_device(): near = jnp.stack((own, lax.ppermute(own, 'yl', SWAP)), 0)]
    pallas_call x2 -> x3, Pallas kernels: 4.4 us -> 6.44 us  [the longest x1 3.97 us: on_device(): pl.pallas_call(exchange_kernel, out_shape=jax.ShapeDtypeStruct((n_far, OW...]
    unnamed x8 -> x6, local copies, waits for them, and re-layouts: 0.01 us -> 1.3 us
  transfers between devices with their start and end apart: 3 -> 8, of which waited for: 3 -> 4; matrix products, arithmetic and copies ran while one was open for 1% -> 3% of each run, Pallas kernels for 0% -> 2%
where the time goes in v3:
time: 92.1 us; the launch traced here: 90.3 us
  starting transfers between devices  39.3 us (43%)
  blocking collectives  29.9 us (32%)
  waiting for transfers between devices  9.7 us (11%)
  Pallas kernels  6.44 us (7%)
  local copies, waits for them, and re-layouts  2.22 us (2%)
  other arithmetic  1.89 us (2%)
    all_to_all x1, blocking collectives, on_device(): arrived = lax.all_to_all(send, FAR, 0, 0, tiled=True)  29.9 us
    all_to_all x1, starting transfers between devices, on_device(): lax.all_to_all(mine, ORB, 0, 0, tiled=True)  12.7 us
    ppermute x1, starting transfers between devices, on_device(): listed_core = lax.ppermute(listed, 'c', SWAP)  5.95 us
    ppermute x1, starting transfers between devices, on_device(): g_side = lax.ppermute(g, 'zl', SWAP)  5.86 us
    ppermute x1, starting transfers between devices, on_device(): g_both = lax.ppermute(g_side, 'c', SWAP)  5.82 us
    ppermute x1, waiting for transfers between devices, on_device(): near = jnp.stack((own, lax.ppermute(own, 'yl', SWAP)), 0)  4.79 us
    pallas_call x1, Pallas kernels, on_device(): pl.pallas_call(exchange_kernel, out_shape=jax.ShapeDtypeStruct((n_far, OW...  3.97 us
    ppermute x1, waiting for transfers between devices, on_device(): listed = jnp.concatenate((listed, lax.ppermute(listed, 'zl', SWAP)), 0)  2.83 us
  transfers between devices with their start and end apart: 8, of which 4 were waited for; matrix products, arithmetic and copies ran while one was open for 3% of the time, Pallas kernels for 2%

profile of v3, /device:TPU:1, one launch (start us, length us, event | category | flops | bytes accessed | tf_op | source)
XLA Modules:
  0.0 90.3 jit_solution(6404183461562959523)
XLA Ops:
  0.0 0.0 copy-start
  0.0 5.9 %collective-permute-start.2 = (bf16[2,8,128,256]{3,2,1,0:T(8,128)(2,1)}, bf16[2,8,128,256]{3,2,1,0:T(8,128)(2,1)S(1)}, u32[]{:S(2)}, u32[]{:S(2)}) collective-permute-start(bf16[2,8,128,256]{3,2,1,0:T(8,128)(2,1)} %bitcast.16), channel_id=1, source_target_pairs={{0,2},{2,0},{1,3},{3,1},{4,6},{6,4},{5,7},{7,5},{8,10},{10,8},{9,1... | collective-permute-start | bytes 3145736 | tf_op jit(solution)/shard_map/ppermute | solution.py:101
  5.9 0.7 fusion.1
  6.6 0.9 %broadcast_in_dim.41 = bf16[32,64,128]{2,1,0:T(8,128)(2,1)} broadcast(bf16[64,128]{1,0:T(8,128)(2,1)S(1)} %fusion.1), dimensions={1,2} | broadcast | bytes 540672 | tf_op jit(solution)/shard_map/broadcast_in_dim | solution.py:96
  7.5 12.7 %all-to-all-start = ((bf16[32,64,128]{2,1,0:T(8,128)(2,1)}), bf16[32,64,128]{2,1,0:T(8,128)(2,1)}, u32[]{:S(2)}, u32[]{:S(2)}) async-start(bf16[32,64,128]{2,1,0:T(8,128)(2,1)} %broadcast_in_dim.41), calls=%async_computation | async-start | bytes 1048576 | tf_op jit(solution)/shard_map/all_to_all | solution.py:97
  20.9 0.0 copy-start.1
  20.9 0.6 copy-done.1
  21.6 0.1 select_reduce_fusion.1
  21.7 0.0 copy-start.2
  21.7 0.6 copy-done.2
  22.3 0.1 select_reduce_fusion
  22.4 1.9 %collective-permute-start = (s32[1,64]{1,0:T(1,128)S(1)}, s32[1,64]{1,0:T(1,128)S(1)}, u32[]{:S(2)}, u32[]{:S(2)}) collective-permute-start(s32[1,64]{1,0:T(1,128)S(1)} %bitcast.22), channel_id=1, source_target_pairs={{0,2},{2,0},{1,3},{3,1},{4,6},{6,4},{5,7},{7,5},{8,10},{10,8},{9,1... | collective-permute-start | bytes 776 | tf_op jit(solution)/shard_map/ppermute | solution.py:104
  24.4 2.8 %collective-permute-done = s32[1,64]{1,0:T(1,128)S(1)} collective-permute-done((s32[1,64]{1,0:T(1,128)S(1)}, s32[1,64]{1,0:T(1,128)S(1)}, u32[]{:S(2)}, u32[]{:S(2)}) %collective-permute-start) | collective-permute-done | bytes 288 | tf_op jit(solution)/shard_map/ppermute | solution.py:104
  27.2 6.0 %collective-permute-start.1 = (s32[2,64]{1,0:T(2,128)S(1)}, s32[2,64]{1,0:T(2,128)S(1)}, u32[]{:S(2)}, u32[]{:S(2)}) collective-permute-start(s32[2,64]{1,0:T(2,128)S(1)} %pad_add_fusion.refs_0_), channel_id=1, source_target_pairs={{0,1},{1,0},{2,3},{3,2},{4,5},{5,4},{6,7},{7,6},{8,9},{9,8},{10,11... | collective-permute-start | bytes 1544 | tf_op jit(solution)/shard_map/ppermute | solution.py:105
  33.2 0.0 copy-done
  33.2 1.9 %collective-permute-start.5 = (bf16[2,8,128,256]{3,2,1,0:T(8,128)(2,1)S(1)}, bf16[2,8,128,256]{3,2,1,0:T(8,128)(2,1)S(1)}, u32[]{:S(2)}, u32[]{:S(2)}) collective-permute-start(bf16[2,8,128,256]{3,2,1,0:T(8,128)(2,1)S(1)} %bitcast.17), channel_id=1, source_target_pairs={{0,1},{1,0},{2,3},{3,2},{4,5},{5,4},{6,7},{7,6},{8,9},{9,8},{10,11... | collective-permute-start | bytes 3145736 | tf_op jit(solution)/shard_map/ppermute | solution.py:102
  35.1 0.0 collective-permute-done.1.refs_1_
  35.1 0.9 %all-to-all-done = bf16[32,64,128]{2,1,0:T(8,128)(2,1)} async-done(((bf16[32,64,128]{2,1,0:T(8,128)(2,1)}), bf16[32,64,128]{2,1,0:T(8,128)(2,1)}, u32[]{:S(2)}, u32[]{:S(2)}) %all-to-all-start) | async-done | bytes 524320 | tf_op jit(solution)/shard_map/all_to_all | solution.py:97
  36.1 1.7 %select_columns.1 = bf16[2,32,8,128]{3,2,1,0:T(8,128)(2,1)} custom-call(s32[1,2]{1,0:T(1,128)} %columns.1, bf16[32,8,8,128]{3,2,1,0:T(8,128)(2,1)} %bitcast.7.got), custom_call_target="tpu_custom_call" | custom-call | tf_op jit(solution)/shard_map/select_columns/pallas_call | solution.py:110
  37.8 0.0 collective-permute-done.2.refs_5_
  37.8 5.8 %collective-permute-start.6 = (bf16[2,8,128,256]{3,2,1,0:T(8,128)(2,1)S(1)}, bf16[2,8,128,256]{3,2,1,0:T(8,128)(2,1)S(1)}, u32[]{:S(2)}, u32[]{:S(2)}) collective-permute-start(bf16[2,8,128,256]{3,2,1,0:T(8,128)(2,1)S(1)} %collective-permute-done.2.refs_5_), channel_id=1, source_target_pairs={{0,1},{1,0},{2,3},{3,2},{4,5},{5,4},{6,7},{7,6},{8,9},{9,8},{10,11... | collective-permute-start | bytes 3145736 | tf_op jit(solution)/shard_map/ppermute | solution.py:118
  43.6 2.4 %collective-permute-start.3 = (bf16[2,256,128]{2,1,0:T(8,128)(2,1)}, bf16[2,256,128]{2,1,0:T(8,128)(2,1)S(1)}, u32[]{:S(2)}, u32[]{:S(2)}) collective-permute-start(bf16[2,256,128]{2,1,0:T(8,128)(2,1)} %bitcast.19), channel_id=1, source_target_pairs={{0,16},{16,0},{1,17},{17,1},{2,18},{18,2},{3,19},{19,3},{4,20},{20... | collective-permute-start | bytes 393224 | tf_op jit(solution)/shard_map/ppermute | solution.py:119
  46.1 4.8 %collective-permute-done.3 = bf16[2,256,128]{2,1,0:T(8,128)(2,1)S(1)} collective-permute-done((bf16[2,256,128]{2,1,0:T(8,128)(2,1)}, bf16[2,256,128]{2,1,0:T(8,128)(2,1)S(1)}, u32[]{:S(2)}, u32[]{:S(2)}) %collective-permute-start.3) | collective-permute-done | bytes 131104 | tf_op jit(solution)/shard_map/ppermute | solution.py:119
  50.8 0.9 %pad_maximum_fusion.refs_2_ = bf16[2,2,256,128]{3,2,1,0:T(8,128)(2,1)S(1)} fusion(bf16[1,2,256,128]{3,2,1,0:T(8,128)(2,1)S(1)} %bitcast.21, bf16[1,2,256,128]{3,2,1,0:T(8,128)(2,1)} %bitcast.20), kind=kLoop, calls=%fused_computation | loop fusion | flops 131072 | bytes 524288 | tf_op jit(solution)/shard_map/stack | solution.py:119
  51.8 2.7 %collective-permute-start.4 = (bf16[2,2,256,128]{3,2,1,0:T(8,128)(2,1)S(1)}, bf16[2,2,256,128]{3,2,1,0:T(8,128)(2,1)S(1)}, u32[]{:S(2)}, u32[]{:S(2)}) collective-permute-start(bf16[2,2,256,128]{3,2,1,0:T(8,128)(2,1)S(1)} %pad_maximum_fusion.refs_2_), channel_id=1, source_target_pairs={{0,1},{1,0},{2,3},{3,2},{4,5},{5,4},{6,7},{7,6},{8,9},{9,8},{10,11... | collective-permute-start | bytes 786440 | tf_op jit(solution)/shard_map/ppermute | solution.py:120
  54.5 0.0 collective-permute-done.5.refs_6_
  54.5 1.1 %collective-permute-done.4.refs_3_ = bf16[2,2,256,128]{3,2,1,0:T(8,128)(2,1)S(1)} collective-permute-done((bf16[2,2,256,128]{3,2,1,0:T(8,128)(2,1)S(1)}, bf16[2,2,256,128]{3,2,1,0:T(8,128)(2,1)S(1)}, u32[]{:S(2)}, u32[]{:S(2)}) %collective-permute-start.4) | collective-permute-done | bytes 262176 | tf_op jit(solution)/shard_map/ppermute | solution.py:120
  55.6 0.0 collective-permute-done.6.refs_7_
  55.6 4.0 %exchange_blocks.1 = bf16[8,256,128]{2,1,0:T(8,128)(2,1)S(1)} custom-call(s32[2,64]{1,0:T(2,128)S(1)} %pad_add_fusion.refs_0_, s32[2,64]{1,0:T(2,128)S(1)} %collective-permute-done.1.refs_1_, bf16[2,2,256,128]{3,2,1,0:T(8,128)(2,1)S(1)} %pad_maximum_fusion.refs_2_, bf16[2,2,256,128]{3,2,1,0:T(8,128)(2,1)S(1)} %collective-permute-done.4.refs_3_, ...), custom_call_target="tpu_custom_call" | custom-call | tf_op jit(solution)/shard_map/exchange_blocks/pallas_call | solution.py:123
  59.6 29.9 %all_to_all.10.got = bf16[8,256,128]{2,1,0:T(8,128)(2,1)S(1)} all-to-all(bf16[8,256,128]{2,1,0:T(8,128)(2,1)S(1)} %exchange_blocks.1), channel_id=1, replica_groups=mesh['x'=8,'yh'=4,'yl'=2,'zh'=4,'zl'=2,'c'=2] {'yl','zh'}, dimensions={0} | all-to-all | bytes 1048576 | tf_op jit(solution)/shard_map/all_to_all | solution.py:132
  89.6 0.7 sum_slots.1
  (3 shorter events, 0.0 us)
Async XLA Ops:
  0.0 33.2 %copy-start = (bf16[2,1024,256]{2,1,0:T(8,128)(2,1)S(1)}, bf16[2,1024,256]{2,1,0:T(8,128)(2,1)}, u32[]{:S(2)}) copy-start(bf16[2,1024,256]{2,1,0:T(8,128)(2,1)} %param.7) | copy-start | bytes 3145732
  0.0 37.8 %collective-permute-start.2 = (bf16[2,8,128,256]{3,2,1,0:T(8,128)(2,1)}, bf16[2,8,128,256]{3,2,1,0:T(8,128)(2,1)S(1)}, u32[]{:S(2)}, u32[]{:S(2)}) collective-permute-start(bf16[2,8,128,256]{3,2,1,0:T(8,128)(2,1)} %bitcast.16), channel_id=1, source_target_pairs={{0,2},{2,0},{1,3},{3,1},{4,6},{6,4},{5,7},{7,5},{8,10},{10,8},{9,1... | collective-permute-start | bytes 3145736 | tf_op jit(solution)/shard_map/ppermute | solution.py:101
  7.5 28.5 %all-to-all-start = ((bf16[32,64,128]{2,1,0:T(8,128)(2,1)}), bf16[32,64,128]{2,1,0:T(8,128)(2,1)}, u32[]{:S(2)}, u32[]{:S(2)}) async-start(bf16[32,64,128]{2,1,0:T(8,128)(2,1)} %broadcast_in_dim.41), calls=%async_computation | async-start | bytes 1048576 | tf_op jit(solution)/shard_map/all_to_all | solution.py:97
  20.9 0.7 copy-start.1
  21.7 0.7 copy-start.2
  22.4 4.8 %collective-permute-start = (s32[1,64]{1,0:T(1,128)S(1)}, s32[1,64]{1,0:T(1,128)S(1)}, u32[]{:S(2)}, u32[]{:S(2)}) collective-permute-start(s32[1,64]{1,0:T(1,128)S(1)} %bitcast.22), channel_id=1, source_target_pairs={{0,2},{2,0},{1,3},{3,1},{4,6},{6,4},{5,7},{7,5},{8,10},{10,8},{9,1... | collective-permute-start | bytes 776 | tf_op jit(solution)/shard_map/ppermute | solution.py:104
  27.2 7.9 %collective-permute-start.1 = (s32[2,64]{1,0:T(2,128)S(1)}, s32[2,64]{1,0:T(2,128)S(1)}, u32[]{:S(2)}, u32[]{:S(2)}) collective-permute-start(s32[2,64]{1,0:T(2,128)S(1)} %pad_add_fusion.refs_0_), channel_id=1, source_target_pairs={{0,1},{1,0},{2,3},{3,2},{4,5},{5,4},{6,7},{7,6},{8,9},{9,8},{10,11... | collective-permute-start | bytes 1544 | tf_op jit(solution)/shard_map/ppermute | solution.py:105
  33.2 21.3 %collective-permute-start.5 = (bf16[2,8,128,256]{3,2,1,0:T(8,128)(2,1)S(1)}, bf16[2,8,128,256]{3,2,1,0:T(8,128)(2,1)S(1)}, u32[]{:S(2)}, u32[]{:S(2)}) collective-permute-start(bf16[2,8,128,256]{3,2,1,0:T(8,128)(2,1)S(1)} %bitcast.17), channel_id=1, source_target_pairs={{0,1},{1,0},{2,3},{3,2},{4,5},{5,4},{6,7},{7,6},{8,9},{9,8},{10,11... | collective-permute-start | bytes 3145736 | tf_op jit(solution)/shard_map/ppermute | solution.py:102
  37.8 17.8 %collective-permute-start.6 = (bf16[2,8,128,256]{3,2,1,0:T(8,128)(2,1)S(1)}, bf16[2,8,128,256]{3,2,1,0:T(8,128)(2,1)S(1)}, u32[]{:S(2)}, u32[]{:S(2)}) collective-permute-start(bf16[2,8,128,256]{3,2,1,0:T(8,128)(2,1)S(1)} %collective-permute-done.2.refs_5_), channel_id=1, source_target_pairs={{0,1},{1,0},{2,3},{3,2},{4,5},{5,4},{6,7},{7,6},{8,9},{9,8},{10,11... | collective-permute-start | bytes 3145736 | tf_op jit(solution)/shard_map/ppermute | solution.py:118
  43.6 7.2 %collective-permute-start.3 = (bf16[2,256,128]{2,1,0:T(8,128)(2,1)}, bf16[2,256,128]{2,1,0:T(8,128)(2,1)S(1)}, u32[]{:S(2)}, u32[]{:S(2)}) collective-permute-start(bf16[2,256,128]{2,1,0:T(8,128)(2,1)} %bitcast.19), channel_id=1, source_target_pairs={{0,16},{16,0},{1,17},{17,1},{2,18},{18,2},{3,19},{19,3},{4,20},{20... | collective-permute-start | bytes 393224 | tf_op jit(solution)/shard_map/ppermute | solution.py:119
  51.8 3.9 %collective-permute-start.4 = (bf16[2,2,256,128]{3,2,1,0:T(8,128)(2,1)S(1)}, bf16[2,2,256,128]{3,2,1,0:T(8,128)(2,1)S(1)}, u32[]{:S(2)}, u32[]{:S(2)}) collective-permute-start(bf16[2,2,256,128]{3,2,1,0:T(8,128)(2,1)S(1)} %pad_maximum_fusion.refs_2_), channel_id=1, source_target_pairs={{0,1},{1,0},{2,3},{3,2},{4,5},{5,4},{6,7},{7,6},{8,9},{9,8},{10,11... | collective-permute-start | bytes 786440 | tf_op jit(solution)/shard_map/ppermute | solution.py:120

commit v4 on v3

v4 whole, which is shorter than its diff:
```python
import jax
import jax.numpy as jnp
from jax import lax
from jax.experimental import pallas as pl
from jax.experimental.pallas import tpu as pltpu
from jax.sharding import Mesh, PartitionSpec as P

BLK = 128
NCB = 2
OWN = 2
AUX = 2
TILE = 16
ORB = ("x", "yh")
FAR = ("yl", "zh")
BAS = ("yl", "zh", "zl", "c")
SWAP = ((0, 1), (1, 0))
F32 = jnp.float32
BF16 = jnp.bfloat16


def contract(a, b, da, db):
    return lax.dot_general(a, b, (((da,), (db,)), ((), ())), preferred_element_type=F32)


def prepare_kernel(pairs, count, slots, occ, amp, g_ref, mine, packed):
    half = occ.shape[0] // 2
    tensor = jnp.where(lax.axis_index("yl") == 0, occ[...].astype(F32), amp[...].astype(F32))
    tensor = jnp.where(lax.axis_index("c") == 0, tensor[:half], tensor[half:])
    parts = [tensor[:, n * BLK:(n + 1) * BLK] for n in range(tensor.shape[1] // BLK)]
    block = jnp.concatenate(parts, axis=0).astype(BF16)
    for i in range(mine.shape[0]):
        mine[i] = block

    rows, width = g_ref.shape
    packed[0:rows] = g_ref[...]
    lane = lax.broadcasted_iota(jnp.int32, (TILE, width), 1)
    listed = jnp.full((TILE, width), -1, jnp.int32)
    for e in range(pairs.shape[2]):
        p = pairs[0, 0, e]
        here = jnp.where(e < count[0, 0], slots[0, p], -1)
        listed = jnp.where(lane == here, p, listed)
    packed[rows:rows + TILE] = listed.astype(F32).astype(BF16)


def exchange_kernel(*refs):
    near, far, slabs = refs[0], refs[1], refs[2:6]
    out, t_ref, held, wide_list, listed, sem, held_sem = refs[6:]
    fetches = [pltpu.make_async_copy(slabs[2 + i], held.at[i], held_sem.at[i]) for i in range(2)]
    for fetch in fetches:
        fetch.start()
    slabs = [slabs[0], slabs[1], held.at[0], held.at[1]]
    rows, width = t_ref.shape[1:]
    aux_blocks = rows // BLK
    row_blocks = aux_blocks // AUX

    def wide(t):
        return jnp.concatenate(
            [jnp.concatenate([ref[t, k] for k in range(NCB)], axis=1) for ref in (near, far)], axis=0
        )

    first, second = wide(0), wide(1)
    is_occ = lax.axis_index("yl") == 0
    s = contract(jnp.where(is_occ, first, second), jnp.where(is_occ, second, first), 0, 0)
    s = s.astype(BF16)
    step = 2 * BLK
    for k, g_ref in enumerate(slabs):
        if k >= 2:
            fetches[k - 2].wait()
        wide_list[k] = g_ref[rows:rows + TILE, 0:BLK].astype(F32).astype(jnp.int32)
        if k == 3:
            copy = pltpu.make_async_copy(wide_list, listed, sem)
            copy.start()
        for m in range(0, rows, step):
            t_ref[k, m:m + step] = contract(g_ref[m:m + step], s, 1, 0).astype(BF16)
    copy.wait()

    quarter = lax.axis_index("zl") * 2 + lax.axis_index("c")

    def owner(j, _):
        slot = (j * 4 + quarter) * OWN
        total = [jnp.zeros((BLK, BLK), F32)] * OWN
        for k, g_ref in enumerate(slabs):
            pair = [listed[k, 0, slot + h] for h in range(OWN)]
            p = jnp.maximum(jnp.maximum(pair[0], pair[1]), 0)
            block = None
            for q in range(AUX):
                at = [
                    pl.ds(pl.multiple_of((q * row_blocks + r) * BLK, BLK), BLK)
                    for r in (p // row_blocks, p % row_blocks)
                ]
                term = contract(t_ref[k, at[0]], g_ref[at[1]], 1, 1)
                block = term if block is None else block + term
            total = [total[h] + jnp.where(pair[h] >= 0, block, 0.0) for h in range(OWN)]
        for h in range(OWN):
            out[j, h * BLK:(h + 1) * BLK] = total[h].astype(BF16)
        return 0

    lax.fori_loop(0, out.shape[0], owner, 0, unroll=2)


def select_kernel(columns, got, *rest):
    out = rest[-1]
    for k in range(NCB):
        out[k] = got[:, columns[0, k]]


def sum_kernel(got, out):
    for h in range(OWN):
        total = got[0, h * BLK:(h + 1) * BLK].astype(F32)
        for j in range(1, got.shape[0]):
            total = total + got[j, h * BLK:(h + 1) * BLK].astype(F32)
        out[0, h] = total


def on_device(three_centre, occ_coeff, amp_coeff, col_blocks, slot_map, pair_list, pair_count):
    n_orb = lax.axis_size(ORB)
    n_far = lax.axis_size(FAR)
    own_rows, width = occ_coeff.shape
    half = own_rows // 2
    col_total = width // BLK

    aux, rows, sel = three_centre.shape
    vmem = pl.BlockSpec(memory_space=pltpu.VMEM)
    smem = pl.BlockSpec(memory_space=pltpu.SMEM)
    mine, g = pl.pallas_call(
        prepare_kernel,
        out_shape=(
            jax.ShapeDtypeStruct((n_orb, col_total * half, BLK), BF16),
            jax.ShapeDtypeStruct((aux * rows + TILE, sel), BF16),
        ),
        in_specs=[smem] * 3 + [vmem] * 3,
        out_specs=(vmem, vmem),
        name="prepare",
    )(pair_list, pair_count, slot_map, occ_coeff, amp_coeff, three_centre.reshape(aux * rows, sel))
    with jax.named_scope("g_side"):
        g_side = lax.ppermute(g, "zl", SWAP)
    with jax.named_scope("g_core"):
        g_core = lax.ppermute(g, "c", SWAP)
    with jax.named_scope("g_both"):
        g_both = lax.ppermute(g_side, "c", SWAP)
    got = lax.all_to_all(mine, ORB, 0, 0, tiled=True).reshape(n_orb, col_total, half, BLK)
    own = pl.pallas_call(
        select_kernel,
        out_shape=jax.ShapeDtypeStruct((NCB, n_orb, half, BLK), BF16),
        in_specs=[smem, vmem] + [pl.BlockSpec(memory_space=pl.ANY)] * 0,
        out_specs=vmem,
        compiler_params=pltpu.CompilerParams(vmem_limit_bytes=4 * 1024 * 1024),
        name="select_columns",
    )(col_blocks, got).reshape(NCB, n_orb * half, BLK)
    with jax.named_scope("other"):
        other = lax.ppermute(own, "yl", SWAP)
    near = jnp.stack((own, other), 0)
    with jax.named_scope("far"):
        far = lax.ppermute(near, "c", SWAP)
    coeffs = (near, far)
    slabs = (g, g_side, g_core, g_both)

    send = pl.pallas_call(
        exchange_kernel,
        out_shape=jax.ShapeDtypeStruct((n_far, OWN * BLK, BLK), BF16),
        in_specs=[vmem] * 4 + [pl.BlockSpec(memory_space=pl.ANY)] * 2,
        out_specs=vmem,
        scratch_shapes=[
            pltpu.VMEM((len(slabs), aux * rows, sel), BF16),
            pltpu.VMEM((2,) + g.shape, BF16),
            pltpu.VMEM((len(slabs), TILE, BLK), jnp.int32),
            pltpu.SMEM((len(slabs), TILE, BLK), jnp.int32),
            pltpu.SemaphoreType.DMA,
            pltpu.SemaphoreType.DMA((2,)),
        ],
        compiler_params=pltpu.CompilerParams(vmem_limit_bytes=12 * 1024 * 1024),
        name="exchange_blocks",
    )(*coeffs, *slabs)
    arrived = lax.all_to_all(send, FAR, 0, 0, tiled=True)
    return pl.pallas_call(
        sum_kernel,
        out_shape=jax.ShapeDtypeStruct((1, OWN, BLK, BLK), F32),
        in_specs=[vmem],
        out_specs=vmem,
        compiler_params=pltpu.CompilerParams(vmem_limit_bytes=12 * 1024 * 1024),
        name="sum_slots",
    )(arrived)


def solution(mesh):
    fine = Mesh(mesh.devices.reshape(8, 4, 2, 4, 2, 2), ("x", "yh", "yl", "zh", "zl", "c"))
    placed = (
        P(BAS, ORB, None),
        P(ORB, None),
        P(ORB, None),
        P(ORB, None),
        P(ORB, None),
        P(ORB, BAS, None),
        P(ORB, BAS),
    )
    return jax.shard_map(
        on_device,
        mesh=fine,
        in_specs=placed,
        out_specs=P(ORB, BAS, None, None),
        check_vma=False,
    )
```

time: 92.1 us -> 89.2 us (0.969)
  waiting for transfers between devices: 9.7 us -> 7.15 us
  Pallas kernels: 6.44 us -> 8.81 us
  local copies, waits for them, and re-layouts: 2.22 us -> 0.01 us
  other arithmetic: 1.89 us -> 0.03 us
  starting transfers between devices: 39.3 us -> 40.9 us
    ppermute x3 -> x1, starting transfers between devices: 10.3 us -> 1.92 us  [on_device(): other = lax.ppermute(own, 'yl', SWAP)]
    ppermute x1, starting transfers between devices: 5.82 us -> 11 us  [on_device(): g_both = lax.ppermute(g_side, 'c', SWAP)]
    ppermute x3 -> x1, waiting for transfers between devices: 7.62 us -> 3.78 us  [on_device(): other = lax.ppermute(own, 'yl', SWAP)]
    ppermute x1, starting transfers between devices: 2.7 us -> 5.98 us  [on_device(): far = lax.ppermute(near, 'c', SWAP)]
    pallas_call x0 -> x1, Pallas kernels: none -> 2.56 us  [on_device(): pl.pallas_call(prepare_kernel, out_shape=(jax.ShapeDtypeStruct((n_orb, co...]
    ppermute x1, starting transfers between devices: 1.92 us -> 3.55 us  [on_device(): g_core = lax.ppermute(g, 'c', SWAP)]
    unnamed x6 -> x4, local copies, waits for them, and re-layouts: 1.3 us -> 0.01 us
    all_to_all x1, waiting for transfers between devices: 0.94 us -> 2.23 us  [on_device(): lax.all_to_all(mine, ORB, 0, 0, tiled=True)]
  transfers between devices with their start and end apart: 8 -> 6, of which waited for: 4 -> 3; matrix products, arithmetic and copies ran while one was open for 3% -> 0% of each run, Pallas kernels for 2% -> 1%
where the time goes in v4:
time: 89.2 us; the launch traced here: 87.6 us
  starting transfers between devices  40.9 us (46%)
  blocking collectives  29.9 us (34%)
  Pallas kernels  8.81 us (10%)
  waiting for transfers between devices  7.15 us (8%)
    all_to_all x1, blocking collectives, on_device(): arrived = lax.all_to_all(send, FAR, 0, 0, tiled=True)  29.9 us
    all_to_all x1, starting transfers between devices, on_device(): lax.all_to_all(mine, ORB, 0, 0, tiled=True)  12.7 us
    ppermute x1, starting transfers between devices, on_device(): g_both = lax.ppermute(g_side, 'c', SWAP)  11 us
    ppermute x1, starting transfers between devices, on_device(): far = lax.ppermute(near, 'c', SWAP)  5.98 us
    ppermute x1, starting transfers between devices, on_device(): g_side = lax.ppermute(g, 'zl', SWAP)  5.73 us
    pallas_call x1, Pallas kernels, on_device(): pl.pallas_call(exchange_kernel, out_shape=jax.ShapeDtypeStruct((n_far, OW...  4.95 us
    ppermute x1, waiting for transfers between devices, on_device(): other = lax.ppermute(own, 'yl', SWAP)  3.78 us
    ppermute x1, starting transfers between devices, on_device(): g_core = lax.ppermute(g, 'c', SWAP)  3.55 us
  transfers between devices with their start and end apart: 6, of which 3 were waited for; matrix products, arithmetic and copies ran while one was open for 0% of the time, Pallas kernels for 1%

profile of v4, /device:TPU:1, one launch (start us, length us, event | category | flops | bytes accessed | tf_op | source)
XLA Modules:
  0.0 87.6 jit_solution(7169641046542712375)
XLA Ops:
  0.7 0.0 copy-start.1
  0.7 2.6 %prepare.1 = (bf16[32,64,128]{2,1,0:T(8,128)(2,1)}, bf16[2064,256]{1,0:T(8,128)(2,1)}) custom-call(s32[1,1,32]{2,1,0:T(1,128)} %pairs.1, s32[1,1]{1,0:T(1,128)S(6)} %copy.8.count, s32[1,64]{1,0:T(1,128)} %slots.1, bf16[16,1024]{1,0:T(8,128)(2,1)} %occ.1, bf16[16,1024]{1,0:T(8,128)(2,1)} %amp.1, bf16[2048,256]{1,0:T(8,128)(2,1)} %bitcast.8), custom_call_target="tpu_custom_call" | custom-call | tf_op jit(solution)/shard_map/prepare/pallas_call | solution.py:125
  3.2 5.7 %collective-permute-start.2 = (bf16[2064,256]{1,0:T(8,128)(2,1)}, bf16[2064,256]{1,0:T(8,128)(2,1)S(1)}, u32[]{:S(2)}, u32[]{:S(2)}) collective-permute-start(bf16[2064,256]{1,0:T(8,128)(2,1)} %get-tuple-element.8.refs_2_), channel_id=1, source_target_pairs={{0,2},{2,0},{1,3},{3,1},{4,6},{6,4},{5,7},{7,5},{8,10},{10,8},{9,1... | collective-permute-start | bytes 3170312 | tf_op jit(solution)/shard_map/g_side/ppermute | solution.py:136
  9.0 0.0 copy-start
  9.0 12.7 %all-to-all-start = ((bf16[32,64,128]{2,1,0:T(8,128)(2,1)}), bf16[32,64,128]{2,1,0:T(8,128)(2,1)S(1)}, u32[]{:S(2)}, u32[]{:S(2)}) async-start(bf16[32,64,128]{2,1,0:T(8,128)(2,1)} %get-tuple-element.7), calls=%async_computation | async-start | bytes 1048576 | tf_op jit(solution)/shard_map/all_to_all | solution.py:141
  21.7 3.5 %collective-permute-start.3 = (bf16[2064,256]{1,0:T(8,128)(2,1)}, bf16[2064,256]{1,0:T(8,128)(2,1)}, u32[]{:S(2)}, u32[]{:S(2)}) collective-permute-start(bf16[2064,256]{1,0:T(8,128)(2,1)} %get-tuple-element.8.refs_2_), channel_id=1, source_target_pairs={{0,1},{1,0},{2,3},{3,2},{4,5},{5,4},{6,7},{7,6},{8,9},{9,8},{10,11... | collective-permute-start | bytes 3170312 | tf_op jit(solution)/shard_map/g_core/ppermute | solution.py:138
  25.3 0.0 collective-permute-done.2.refs_3_
  25.3 11.0 %collective-permute-start.4 = (bf16[2064,256]{1,0:T(8,128)(2,1)S(1)}, bf16[2064,256]{1,0:T(8,128)(2,1)}, u32[]{:S(2)}, u32[]{:S(2)}) collective-permute-start(bf16[2064,256]{1,0:T(8,128)(2,1)S(1)} %collective-permute-done.2.refs_3_), channel_id=1, source_target_pairs={{0,1},{1,0},{2,3},{3,2},{4,5},{5,4},{6,7},{7,6},{8,9},{9,8},{10,11... | collective-permute-start | bytes 3170312 | tf_op jit(solution)/shard_map/g_both/ppermute | solution.py:140
  36.3 2.2 %all-to-all-done = bf16[32,64,128]{2,1,0:T(8,128)(2,1)S(1)} async-done(((bf16[32,64,128]{2,1,0:T(8,128)(2,1)}), bf16[32,64,128]{2,1,0:T(8,128)(2,1)S(1)}, u32[]{:S(2)}, u32[]{:S(2)}) %all-to-all-start) | async-done | bytes 524320 | tf_op jit(solution)/shard_map/all_to_all | solution.py:141
  38.5 0.0 copy-done.1
  38.5 0.6 select_columns.1
  39.1 1.9 %collective-permute-start = (bf16[2,256,128]{2,1,0:T(8,128)(2,1)S(1)}, bf16[2,256,128]{2,1,0:T(8,128)(2,1)S(1)}, u32[]{:S(2)}, u32[]{:S(2)}) collective-permute-start(bf16[2,256,128]{2,1,0:T(8,128)(2,1)S(1)} %bitcast.6), channel_id=1, source_target_pairs={{0,16},{16,0},{1,17},{17,1},{2,18},{18,2},{3,19},{19,3},{4,20},{20... | collective-permute-start | bytes 393224 | tf_op jit(solution)/shard_map/other/ppermute | solution.py:151
  41.0 3.8 %collective-permute-done = bf16[2,256,128]{2,1,0:T(8,128)(2,1)S(1)} collective-permute-done((bf16[2,256,128]{2,1,0:T(8,128)(2,1)S(1)}, bf16[2,256,128]{2,1,0:T(8,128)(2,1)S(1)}, u32[]{:S(2)}, u32[]{:S(2)}) %collective-permute-start) | collective-permute-done | bytes 131104 | tf_op jit(solution)/shard_map/other/ppermute | solution.py:151
  44.8 6.0 %collective-permute-start.1 = (bf16[2,2,256,128]{3,2,1,0:T(8,128)(2,1)S(1)}, bf16[2,2,256,128]{3,2,1,0:T(8,128)(2,1)S(1)}, u32[]{:S(2)}, u32[]{:S(2)}) collective-permute-start(bf16[2,2,256,128]{3,2,1,0:T(8,128)(2,1)S(1)} %pad_maximum_fusion.refs_0_), channel_id=1, source_target_pairs={{0,1},{1,0},{2,3},{3,2},{4,5},{5,4},{6,7},{7,6},{8,9},{9,8},{10,11... | collective-permute-start | bytes 786440 | tf_op jit(solution)/shard_map/far/ppermute | solution.py:154
  50.8 0.0 collective-permute-done.3.refs_4_
  50.8 1.1 %collective-permute-done.1.refs_1_ = bf16[2,2,256,128]{3,2,1,0:T(8,128)(2,1)S(1)} collective-permute-done((bf16[2,2,256,128]{3,2,1,0:T(8,128)(2,1)S(1)}, bf16[2,2,256,128]{3,2,1,0:T(8,128)(2,1)S(1)}, u32[]{:S(2)}, u32[]{:S(2)}) %collective-permute-start.1) | collective-permute-done | bytes 262176 | tf_op jit(solution)/shard_map/far/ppermute | solution.py:154
  52.0 0.0 collective-permute-done.4.refs_5_
  52.0 0.0 copy-done
  52.0 5.0 %exchange_blocks.1 = bf16[8,256,128]{2,1,0:T(8,128)(2,1)S(1)} custom-call(bf16[2,2,256,128]{3,2,1,0:T(8,128)(2,1)S(1)} %pad_maximum_fusion.refs_0_, bf16[2,2,256,128]{3,2,1,0:T(8,128)(2,1)S(1)} %collective-permute-done.1.refs_1_, bf16[2064,256]{1,0:T(8,128)(2,1)S(1)} %copy-done, bf16[2064,256]{1,0:T(8,128)(2,1)S(1)} %collective-permute-done.2.refs_3_, ...), custom_call_target="tpu_custom_call" | custom-call | tf_op jit(solution)/shard_map/exchange_blocks/pallas_call | solution.py:158
  56.9 29.9 %all_to_all.10.got = bf16[8,256,128]{2,1,0:T(8,128)(2,1)S(1)} all-to-all(bf16[8,256,128]{2,1,0:T(8,128)(2,1)S(1)} %exchange_blocks.1), channel_id=1, replica_groups=mesh['x'=8,'yh'=4,'yl'=2,'zh'=4,'zl'=2,'c'=2] {'yl','zh'}, dimensions={0} | all-to-all | bytes 1048576 | tf_op jit(solution)/shard_map/all_to_all | solution.py:174
  86.9 0.7 sum_slots.1
  (1 shorter events, 0.0 us)
Async XLA Ops:
  0.7 37.8 %copy-start.1 = (s32[1,2]{1,0:T(1,128)S(1)}, s32[1,2]{1,0:T(1,128)}, u32[]{:S(2)}) copy-start(s32[1,2]{1,0:T(1,128)} %columns.1) | copy-start | bytes 28
  3.2 22.0 %collective-permute-start.2 = (bf16[2064,256]{1,0:T(8,128)(2,1)}, bf16[2064,256]{1,0:T(8,128)(2,1)S(1)}, u32[]{:S(2)}, u32[]{:S(2)}) collective-permute-start(bf16[2064,256]{1,0:T(8,128)(2,1)} %get-tuple-element.8.refs_2_), channel_id=1, source_target_pairs={{0,2},{2,0},{1,3},{3,1},{4,6},{6,4},{5,7},{7,5},{8,10},{10,8},{9,1... | collective-permute-start | bytes 3170312 | tf_op jit(solution)/shard_map/g_side/ppermute | solution.py:136
  9.0 43.0 %copy-start = (bf16[2064,256]{1,0:T(8,128)(2,1)S(1)}, bf16[2064,256]{1,0:T(8,128)(2,1)}, u32[]{:S(2)}) copy-start(bf16[2064,256]{1,0:T(8,128)(2,1)} %get-tuple-element.8.refs_2_) | copy-start | bytes 3170308
  9.0 29.5 %all-to-all-start = ((bf16[32,64,128]{2,1,0:T(8,128)(2,1)}), bf16[32,64,128]{2,1,0:T(8,128)(2,1)S(1)}, u32[]{:S(2)}, u32[]{:S(2)}) async-start(bf16[32,64,128]{2,1,0:T(8,128)(2,1)} %get-tuple-element.7), calls=%async_computation | async-start | bytes 1048576 | tf_op jit(solution)/shard_map/all_to_all | solution.py:141
  21.7 29.1 %collective-permute-start.3 = (bf16[2064,256]{1,0:T(8,128)(2,1)}, bf16[2064,256]{1,0:T(8,128)(2,1)}, u32[]{:S(2)}, u32[]{:S(2)}) collective-permute-start(bf16[2064,256]{1,0:T(8,128)(2,1)} %get-tuple-element.8.refs_2_), channel_id=1, source_target_pairs={{0,1},{1,0},{2,3},{3,2},{4,5},{5,4},{6,7},{7,6},{8,9},{9,8},{10,11... | collective-permute-start | bytes 3170312 | tf_op jit(solution)/shard_map/g_core/ppermute | solution.py:138
  25.3 26.7 %collective-permute-start.4 = (bf16[2064,256]{1,0:T(8,128)(2,1)S(1)}, bf16[2064,256]{1,0:T(8,128)(2,1)}, u32[]{:S(2)}, u32[]{:S(2)}) collective-permute-start(bf16[2064,256]{1,0:T(8,128)(2,1)S(1)} %collective-permute-done.2.refs_3_), channel_id=1, source_target_pairs={{0,1},{1,0},{2,3},{3,2},{4,5},{5,4},{6,7},{7,6},{8,9},{9,8},{10,11... | collective-permute-start | bytes 3170312 | tf_op jit(solution)/shard_map/g_both/ppermute | solution.py:140
  39.1 5.7 %collective-permute-start = (bf16[2,256,128]{2,1,0:T(8,128)(2,1)S(1)}, bf16[2,256,128]{2,1,0:T(8,128)(2,1)S(1)}, u32[]{:S(2)}, u32[]{:S(2)}) collective-permute-start(bf16[2,256,128]{2,1,0:T(8,128)(2,1)S(1)} %bitcast.6), channel_id=1, source_target_pairs={{0,16},{16,0},{1,17},{17,1},{2,18},{18,2},{3,19},{19,3},{4,20},{20... | collective-permute-start | bytes 393224 | tf_op jit(solution)/shard_map/other/ppermute | solution.py:151
  44.8 7.1 %collective-permute-start.1 = (bf16[2,2,256,128]{3,2,1,0:T(8,128)(2,1)S(1)}, bf16[2,2,256,128]{3,2,1,0:T(8,128)(2,1)S(1)}, u32[]{:S(2)}, u32[]{:S(2)}) collective-permute-start(bf16[2,2,256,128]{3,2,1,0:T(8,128)(2,1)S(1)} %pad_maximum_fusion.refs_0_), channel_id=1, source_target_pairs={{0,1},{1,0},{2,3},{3,2},{4,5},{5,4},{6,7},{7,6},{8,9},{9,8},{10,11... | collective-permute-start | bytes 786440 | tf_op jit(solution)/shard_map/far/ppermute | solution.py:154

commit v5 on v4

--- a/solution.py
+++ b/solution.py
@@ -95,7 +95,7 @@
             out[j, h * BLK:(h + 1) * BLK] = total[h].astype(BF16)
         return 0
 
-    lax.fori_loop(0, out.shape[0], owner, 0, unroll=2)
+    lax.fori_loop(0, out.shape[0], owner, 0, unroll=True)
 
 
 def select_kernel(columns, got, *rest):

time: 89.2 us -> 88.6 us (level)
  no operation moved by 1% of the time
where the time goes in v5:
time: 88.6 us; the launch traced here: 87.1 us
  starting transfers between devices  40.9 us (46%)
  blocking collectives  30 us (34%)
  Pallas kernels  8.28 us (9%)
  waiting for transfers between devices  7.15 us (8%)
    all_to_all x1, blocking collectives, on_device(): arrived = lax.all_to_all(send, FAR, 0, 0, tiled=True)  30 us
    all_to_all x1, starting transfers between devices, on_device(): lax.all_to_all(mine, ORB, 0, 0, tiled=True)  12.7 us
    ppermute x1, starting transfers between devices, on_device(): g_both = lax.ppermute(g_side, 'c', SWAP)  11 us
    ppermute x1, starting transfers between devices, on_device(): far = lax.ppermute(near, 'c', SWAP)  5.98 us
    ppermute x1, starting transfers between devices, on_device(): g_side = lax.ppermute(g, 'zl', SWAP)  5.73 us
    pallas_call x1, Pallas kernels, on_device(): pl.pallas_call(exchange_kernel, out_shape=jax.ShapeDtypeStruct((n_far, OW...  4.42 us
    ppermute x1, waiting for transfers between devices, on_device(): other = lax.ppermute(own, 'yl', SWAP)  3.78 us
    ppermute x1, starting transfers between devices, on_device(): g_core = lax.ppermute(g, 'c', SWAP)  3.55 us
  transfers between devices with their start and end apart: 6, of which 3 were waited for; matrix products, arithmetic and copies ran while one was open for 0% of the time, Pallas kernels for 1%

profile of v5, /device:TPU:1, one launch (start us, length us, event | category | flops | bytes accessed | tf_op | source)
XLA Modules:
  0.0 87.1 jit_solution(17866370826959627354)
XLA Ops:
  0.7 0.0 copy-start.1
  0.7 2.6 %prepare.1 = (bf16[32,64,128]{2,1,0:T(8,128)(2,1)}, bf16[2064,256]{1,0:T(8,128)(2,1)}) custom-call(s32[1,1,32]{2,1,0:T(1,128)} %pairs.1, s32[1,1]{1,0:T(1,128)S(6)} %copy.8.count, s32[1,64]{1,0:T(1,128)} %slots.1, bf16[16,1024]{1,0:T(8,128)(2,1)} %occ.1, bf16[16,1024]{1,0:T(8,128)(2,1)} %amp.1, bf16[2048,256]{1,0:T(8,128)(2,1)} %bitcast.8), custom_call_target="tpu_custom_call" | custom-call | tf_op jit(solution)/shard_map/prepare/pallas_call | solution.py:125
  3.2 5.7 %collective-permute-start.2 = (bf16[2064,256]{1,0:T(8,128)(2,1)}, bf16[2064,256]{1,0:T(8,128)(2,1)S(1)}, u32[]{:S(2)}, u32[]{:S(2)}) collective-permute-start(bf16[2064,256]{1,0:T(8,128)(2,1)} %get-tuple-element.8.refs_2_), channel_id=1, source_target_pairs={{0,2},{2,0},{1,3},{3,1},{4,6},{6,4},{5,7},{7,5},{8,10},{10,8},{9,1... | collective-permute-start | bytes 3170312 | tf_op jit(solution)/shard_map/g_side/ppermute | solution.py:136
  9.0 0.0 copy-start
  9.0 12.7 %all-to-all-start = ((bf16[32,64,128]{2,1,0:T(8,128)(2,1)}), bf16[32,64,128]{2,1,0:T(8,128)(2,1)S(1)}, u32[]{:S(2)}, u32[]{:S(2)}) async-start(bf16[32,64,128]{2,1,0:T(8,128)(2,1)} %get-tuple-element.7), calls=%async_computation | async-start | bytes 1048576 | tf_op jit(solution)/shard_map/all_to_all | solution.py:141
  21.7 3.5 %collective-permute-start.3 = (bf16[2064,256]{1,0:T(8,128)(2,1)}, bf16[2064,256]{1,0:T(8,128)(2,1)}, u32[]{:S(2)}, u32[]{:S(2)}) collective-permute-start(bf16[2064,256]{1,0:T(8,128)(2,1)} %get-tuple-element.8.refs_2_), channel_id=1, source_target_pairs={{0,1},{1,0},{2,3},{3,2},{4,5},{5,4},{6,7},{7,6},{8,9},{9,8},{10,11... | collective-permute-start | bytes 3170312 | tf_op jit(solution)/shard_map/g_core/ppermute | solution.py:138
  25.3 0.0 collective-permute-done.2.refs_3_
  25.3 11.0 %collective-permute-start.4 = (bf16[2064,256]{1,0:T(8,128)(2,1)S(1)}, bf16[2064,256]{1,0:T(8,128)(2,1)}, u32[]{:S(2)}, u32[]{:S(2)}) collective-permute-start(bf16[2064,256]{1,0:T(8,128)(2,1)S(1)} %collective-permute-done.2.refs_3_), channel_id=1, source_target_pairs={{0,1},{1,0},{2,3},{3,2},{4,5},{5,4},{6,7},{7,6},{8,9},{9,8},{10,11... | collective-permute-start | bytes 3170312 | tf_op jit(solution)/shard_map/g_both/ppermute | solution.py:140
  36.3 2.2 %all-to-all-done = bf16[32,64,128]{2,1,0:T(8,128)(2,1)S(1)} async-done(((bf16[32,64,128]{2,1,0:T(8,128)(2,1)}), bf16[32,64,128]{2,1,0:T(8,128)(2,1)S(1)}, u32[]{:S(2)}, u32[]{:S(2)}) %all-to-all-start) | async-done | bytes 524320 | tf_op jit(solution)/shard_map/all_to_all | solution.py:141
  38.5 0.0 copy-done.1
  38.5 0.6 select_columns.1
  39.1 1.9 %collective-permute-start = (bf16[2,256,128]{2,1,0:T(8,128)(2,1)S(1)}, bf16[2,256,128]{2,1,0:T(8,128)(2,1)S(1)}, u32[]{:S(2)}, u32[]{:S(2)}) collective-permute-start(bf16[2,256,128]{2,1,0:T(8,128)(2,1)S(1)} %bitcast.6), channel_id=1, source_target_pairs={{0,16},{16,0},{1,17},{17,1},{2,18},{18,2},{3,19},{19,3},{4,20},{20... | collective-permute-start | bytes 393224 | tf_op jit(solution)/shard_map/other/ppermute | solution.py:151
  41.0 3.8 %collective-permute-done = bf16[2,256,128]{2,1,0:T(8,128)(2,1)S(1)} collective-permute-done((bf16[2,256,128]{2,1,0:T(8,128)(2,1)S(1)}, bf16[2,256,128]{2,1,0:T(8,128)(2,1)S(1)}, u32[]{:S(2)}, u32[]{:S(2)}) %collective-permute-start) | collective-permute-done | bytes 131104 | tf_op jit(solution)/shard_map/other/ppermute | solution.py:151
  44.8 6.0 %collective-permute-start.1 = (bf16[2,2,256,128]{3,2,1,0:T(8,128)(2,1)S(1)}, bf16[2,2,256,128]{3,2,1,0:T(8,128)(2,1)S(1)}, u32[]{:S(2)}, u32[]{:S(2)}) collective-permute-start(bf16[2,2,256,128]{3,2,1,0:T(8,128)(2,1)S(1)} %pad_maximum_fusion.refs_0_), channel_id=1, source_target_pairs={{0,1},{1,0},{2,3},{3,2},{4,5},{5,4},{6,7},{7,6},{8,9},{9,8},{10,11... | collective-permute-start | bytes 786440 | tf_op jit(solution)/shard_map/far/ppermute | solution.py:154
  50.8 0.0 collective-permute-done.3.refs_4_
  50.8 1.1 %collective-permute-done.1.refs_1_ = bf16[2,2,256,128]{3,2,1,0:T(8,128)(2,1)S(1)} collective-permute-done((bf16[2,2,256,128]{3,2,1,0:T(8,128)(2,1)S(1)}, bf16[2,2,256,128]{3,2,1,0:T(8,128)(2,1)S(1)}, u32[]{:S(2)}, u32[]{:S(2)}) %collective-permute-start.1) | collective-permute-done | bytes 262176 | tf_op jit(solution)/shard_map/far/ppermute | solution.py:154
  52.0 0.0 collective-permute-done.4.refs_5_
  52.0 0.0 copy-done
  52.0 4.4 %exchange_blocks.1 = bf16[8,256,128]{2,1,0:T(8,128)(2,1)S(1)} custom-call(bf16[2,2,256,128]{3,2,1,0:T(8,128)(2,1)S(1)} %pad_maximum_fusion.refs_0_, bf16[2,2,256,128]{3,2,1,0:T(8,128)(2,1)S(1)} %collective-permute-done.1.refs_1_, bf16[2064,256]{1,0:T(8,128)(2,1)S(1)} %copy-done, bf16[2064,256]{1,0:T(8,128)(2,1)S(1)} %collective-permute-done.2.refs_3_, ...), custom_call_target="tpu_custom_call" | custom-call | tf_op jit(solution)/shard_map/exchange_blocks/pallas_call | solution.py:158
  56.4 30.0 %all_to_all.10.got = bf16[8,256,128]{2,1,0:T(8,128)(2,1)S(1)} all-to-all(bf16[8,256,128]{2,1,0:T(8,128)(2,1)S(1)} %exchange_blocks.1), channel_id=1, replica_groups=mesh['x'=8,'yh'=4,'yl'=2,'zh'=4,'zl'=2,'c'=2] {'yl','zh'}, dimensions={0} | all-to-all | bytes 1048576 | tf_op jit(solution)/shard_map/all_to_all | solution.py:174
  86.4 0.7 sum_slots.1
  (1 shorter events, 0.0 us)
Async XLA Ops:
  0.7 37.8 %copy-start.1 = (s32[1,2]{1,0:T(1,128)S(1)}, s32[1,2]{1,0:T(1,128)}, u32[]{:S(2)}) copy-start(s32[1,2]{1,0:T(1,128)} %columns.1) | copy-start | bytes 28
  3.2 22.0 %collective-permute-start.2 = (bf16[2064,256]{1,0:T(8,128)(2,1)}, bf16[2064,256]{1,0:T(8,128)(2,1)S(1)}, u32[]{:S(2)}, u32[]{:S(2)}) collective-permute-start(bf16[2064,256]{1,0:T(8,128)(2,1)} %get-tuple-element.8.refs_2_), channel_id=1, source_target_pairs={{0,2},{2,0},{1,3},{3,1},{4,6},{6,4},{5,7},{7,5},{8,10},{10,8},{9,1... | collective-permute-start | bytes 3170312 | tf_op jit(solution)/shard_map/g_side/ppermute | solution.py:136
  9.0 43.0 %copy-start = (bf16[2064,256]{1,0:T(8,128)(2,1)S(1)}, bf16[2064,256]{1,0:T(8,128)(2,1)}, u32[]{:S(2)}) copy-start(bf16[2064,256]{1,0:T(8,128)(2,1)} %get-tuple-element.8.refs_2_) | copy-start | bytes 3170308
  9.0 29.5 %all-to-all-start = ((bf16[32,64,128]{2,1,0:T(8,128)(2,1)}), bf16[32,64,128]{2,1,0:T(8,128)(2,1)S(1)}, u32[]{:S(2)}, u32[]{:S(2)}) async-start(bf16[32,64,128]{2,1,0:T(8,128)(2,1)} %get-tuple-element.7), calls=%async_computation | async-start | bytes 1048576 | tf_op jit(solution)/shard_map/all_to_all | solution.py:141
  21.7 29.1 %collective-permute-start.3 = (bf16[2064,256]{1,0:T(8,128)(2,1)}, bf16[2064,256]{1,0:T(8,128)(2,1)}, u32[]{:S(2)}, u32[]{:S(2)}) collective-permute-start(bf16[2064,256]{1,0:T(8,128)(2,1)} %get-tuple-element.8.refs_2_), channel_id=1, source_target_pairs={{0,1},{1,0},{2,3},{3,2},{4,5},{5,4},{6,7},{7,6},{8,9},{9,8},{10,11... | collective-permute-start | bytes 3170312 | tf_op jit(solution)/shard_map/g_core/ppermute | solution.py:138
  25.3 26.7 %collective-permute-start.4 = (bf16[2064,256]{1,0:T(8,128)(2,1)S(1)}, bf16[2064,256]{1,0:T(8,128)(2,1)}, u32[]{:S(2)}, u32[]{:S(2)}) collective-permute-start(bf16[2064,256]{1,0:T(8,128)(2,1)S(1)} %collective-permute-done.2.refs_3_), channel_id=1, source_target_pairs={{0,1},{1,0},{2,3},{3,2},{4,5},{5,4},{6,7},{7,6},{8,9},{9,8},{10,11... | collective-permute-start | bytes 3170312 | tf_op jit(solution)/shard_map/g_both/ppermute | solution.py:140
  39.1 5.7 %collective-permute-start = (bf16[2,256,128]{2,1,0:T(8,128)(2,1)S(1)}, bf16[2,256,128]{2,1,0:T(8,128)(2,1)S(1)}, u32[]{:S(2)}, u32[]{:S(2)}) collective-permute-start(bf16[2,256,128]{2,1,0:T(8,128)(2,1)S(1)} %bitcast.6), channel_id=1, source_target_pairs={{0,16},{16,0},{1,17},{17,1},{2,18},{18,2},{3,19},{19,3},{4,20},{20... | collective-permute-start | bytes 393224 | tf_op jit(solution)/shard_map/other/ppermute | solution.py:151
  44.8 7.1 %collective-permute-start.1 = (bf16[2,2,256,128]{3,2,1,0:T(8,128)(2,1)S(1)}, bf16[2,2,256,128]{3,2,1,0:T(8,128)(2,1)S(1)}, u32[]{:S(2)}, u32[]{:S(2)}) collective-permute-start(bf16[2,2,256,128]{3,2,1,0:T(8,128)(2,1)S(1)} %pad_maximum_fusion.refs_0_), channel_id=1, source_target_pairs={{0,1},{1,0},{2,3},{3,2},{4,5},{5,4},{6,7},{7,6},{8,9},{9,8},{10,11... | collective-permute-start | bytes 786440 | tf_op jit(solution)/shard_map/far/ppermute | solution.py:154

commit v6 on v5

--- a/solution.py
+++ b/solution.py
@@ -43,8 +43,8 @@
 
 
 def exchange_kernel(*refs):
-    near, far, slabs = refs[0], refs[1], refs[2:6]
-    out, t_ref, held, wide_list, listed, sem, held_sem = refs[6:]
+    coeffs, slabs = refs[0:4], refs[4:8]
+    out, t_ref, held, wide_list, listed, sem, held_sem = refs[8:]
     fetches = [pltpu.make_async_copy(slabs[2 + i], held.at[i], held_sem.at[i]) for i in range(2)]
     for fetch in fetches:
         fetch.start()
@@ -53,12 +53,12 @@
     aux_blocks = rows // BLK
     row_blocks = aux_blocks // AUX
 
-    def wide(t):
+    def wide(parts):
         return jnp.concatenate(
-            [jnp.concatenate([ref[t, k] for k in range(NCB)], axis=1) for ref in (near, far)], axis=0
+            [jnp.concatenate([ref[k] for k in range(NCB)], axis=1) for ref in parts], axis=0
         )
 
-    first, second = wide(0), wide(1)
+    first, second = wide(coeffs[0:2]), wide(coeffs[2:4])
     is_occ = lax.axis_index("yl") == 0
     s = contract(jnp.where(is_occ, first, second), jnp.where(is_occ, second, first), 0, 0)
     s = s.astype(BF16)
@@ -149,16 +149,14 @@
     )(col_blocks, got).reshape(NCB, n_orb * half, BLK)
     with jax.named_scope("other"):
         other = lax.ppermute(own, "yl", SWAP)
-    near = jnp.stack((own, other), 0)
-    with jax.named_scope("far"):
-        far = lax.ppermute(near, "c", SWAP)
-    coeffs = (near, far)
+    own_far = lax.ppermute(own, "c", SWAP)
+    coeffs = (own, own_far, other, lax.ppermute(other, "c", SWAP))
     slabs = (g, g_side, g_core, g_both)
 
     send = pl.pallas_call(
         exchange_kernel,
         out_shape=jax.ShapeDtypeStruct((n_far, OWN * BLK, BLK), BF16),
-        in_specs=[vmem] * 4 + [pl.BlockSpec(memory_space=pl.ANY)] * 2,
+        in_specs=[vmem] * (len(coeffs) + 2) + [pl.BlockSpec(memory_space=pl.ANY)] * 2,
         out_specs=vmem,
         scratch_shapes=[
             pltpu.VMEM((len(slabs), aux * rows, sel), BF16),

time: 88.6 us -> 88.4 us (level)
  waiting for transfers between devices: 7.15 us -> 3.05 us
  starting transfers between devices: 40.9 us -> 44.8 us
    ppermute x1, waiting for transfers between devices: 3.78 us -> 0.01 us  [on_device(): other = lax.ppermute(own, 'yl', SWAP)]
    ppermute x1 -> x2, starting transfers between devices: 5.98 us -> 9.73 us  [the longest x1 5.55 us: on_device(): own_far = lax.ppermute(own, 'c', SWAP)]
  transfers between devices with their start and end apart: 6 -> 7, of which waited for: 3 -> 2; matrix products, arithmetic and copies ran while one was open for 0% -> 0% of each run, Pallas kernels for 1% -> 1%
where the time goes in v6:
time: 88.4 us; the launch traced here: 86.8 us
  starting transfers between devices  44.8 us (51%)
  blocking collectives  30 us (34%)
  Pallas kernels  8.27 us (9%)
  waiting for transfers between devices  3.05 us (3%)
    all_to_all x1, blocking collectives, on_device(): arrived = lax.all_to_all(send, FAR, 0, 0, tiled=True)  30 us
    all_to_all x1, starting transfers between devices, on_device(): lax.all_to_all(mine, ORB, 0, 0, tiled=True)  12.6 us
    ppermute x1, starting transfers between devices, on_device(): g_both = lax.ppermute(g_side, 'c', SWAP)  11.1 us
    ppermute x1, starting transfers between devices, on_device(): g_side = lax.ppermute(g, 'zl', SWAP)  5.86 us
    ppermute x1, starting transfers between devices, on_device(): own_far = lax.ppermute(own, 'c', SWAP)  5.55 us
    pallas_call x1, Pallas kernels, on_device(): pl.pallas_call(exchange_kernel, out_shape=jax.ShapeDtypeStruct((n_far, OW...  4.41 us
    ppermute x1, starting transfers between devices, on_device(): coeffs = (own, own_far, other, lax.ppermute(other, 'c', SWAP))  4.18 us
    ppermute x1, starting transfers between devices, on_device(): g_core = lax.ppermute(g, 'c', SWAP)  3.55 us
  transfers between devices with their start and end apart: 7, of which 2 were waited for; matrix products, arithmetic and copies ran while one was open for 0% of the time, Pallas kernels for 1%

profile of v6, /device:TPU:1, one launch (start us, length us, event | category | flops | bytes accessed | tf_op | source)
XLA Modules:
  0.0 86.8 jit_solution(5860990156769491354)
XLA Ops:
  0.7 0.0 copy-start.1
  0.7 2.6 %prepare.1 = (bf16[32,64,128]{2,1,0:T(8,128)(2,1)}, bf16[2064,256]{1,0:T(8,128)(2,1)}) custom-call(s32[1,1,32]{2,1,0:T(1,128)} %pairs.1, s32[1,1]{1,0:T(1,128)S(6)} %copy.8.count, s32[1,64]{1,0:T(1,128)} %slots.1, bf16[16,1024]{1,0:T(8,128)(2,1)} %occ.1, bf16[16,1024]{1,0:T(8,128)(2,1)} %amp.1, bf16[2048,256]{1,0:T(8,128)(2,1)} %bitcast.7), custom_call_target="tpu_custom_call" | custom-call | tf_op jit(solution)/shard_map/prepare/pallas_call | solution.py:125
  3.2 0.0 copy-start
  3.2 5.9 %collective-permute-start.3 = (bf16[2064,256]{1,0:T(8,128)(2,1)}, bf16[2064,256]{1,0:T(8,128)(2,1)S(1)}, u32[]{:S(2)}, u32[]{:S(2)}) collective-permute-start(bf16[2064,256]{1,0:T(8,128)(2,1)} %get-tuple-element.8.refs_4_), channel_id=1, source_target_pairs={{0,2},{2,0},{1,3},{3,1},{4,6},{6,4},{5,7},{7,5},{8,10},{10,8},{9,1... | collective-permute-start | bytes 3170312 | tf_op jit(solution)/shard_map/g_side/ppermute | solution.py:136
  9.1 12.6 %all-to-all-start = ((bf16[32,64,128]{2,1,0:T(8,128)(2,1)}), bf16[32,64,128]{2,1,0:T(8,128)(2,1)S(1)}, u32[]{:S(2)}, u32[]{:S(2)}) async-start(bf16[32,64,128]{2,1,0:T(8,128)(2,1)} %get-tuple-element.7), calls=%async_computation | async-start | bytes 1048576 | tf_op jit(solution)/shard_map/all_to_all | solution.py:141
  21.7 3.5 %collective-permute-start.4 = (bf16[2064,256]{1,0:T(8,128)(2,1)}, bf16[2064,256]{1,0:T(8,128)(2,1)}, u32[]{:S(2)}, u32[]{:S(2)}) collective-permute-start(bf16[2064,256]{1,0:T(8,128)(2,1)} %get-tuple-element.8.refs_4_), channel_id=1, source_target_pairs={{0,1},{1,0},{2,3},{3,2},{4,5},{5,4},{6,7},{7,6},{8,9},{9,8},{10,11... | collective-permute-start | bytes 3170312 | tf_op jit(solution)/shard_map/g_core/ppermute | solution.py:138
  25.2 0.0 collective-permute-done.3.refs_5_
  25.3 11.1 %collective-permute-start.5 = (bf16[2064,256]{1,0:T(8,128)(2,1)S(1)}, bf16[2064,256]{1,0:T(8,128)(2,1)}, u32[]{:S(2)}, u32[]{:S(2)}) collective-permute-start(bf16[2064,256]{1,0:T(8,128)(2,1)S(1)} %collective-permute-done.3.refs_5_), channel_id=1, source_target_pairs={{0,1},{1,0},{2,3},{3,2},{4,5},{5,4},{6,7},{7,6},{8,9},{9,8},{10,11... | collective-permute-start | bytes 3170312 | tf_op jit(solution)/shard_map/g_both/ppermute | solution.py:140
  36.4 2.1 %all-to-all-done = bf16[32,64,128]{2,1,0:T(8,128)(2,1)S(1)} async-done(((bf16[32,64,128]{2,1,0:T(8,128)(2,1)}), bf16[32,64,128]{2,1,0:T(8,128)(2,1)S(1)}, u32[]{:S(2)}, u32[]{:S(2)}) %all-to-all-start) | async-done | bytes 524320 | tf_op jit(solution)/shard_map/all_to_all | solution.py:141
  38.5 0.0 copy-done.1
  38.5 0.6 select_columns.1
  39.1 1.9 %collective-permute-start.1 = (bf16[2,256,128]{2,1,0:T(8,128)(2,1)S(1)}, bf16[2,256,128]{2,1,0:T(8,128)(2,1)S(1)}, u32[]{:S(2)}, u32[]{:S(2)}) collective-permute-start(bf16[2,256,128]{2,1,0:T(8,128)(2,1)S(1)} %bitcast.4), channel_id=1, source_target_pairs={{0,16},{16,0},{1,17},{17,1},{2,18},{18,2},{3,19},{19,3},{4,20},{20... | collective-permute-start | bytes 393224 | tf_op jit(solution)/shard_map/other/ppermute | solution.py:151
  41.0 5.6 %collective-permute-start = (bf16[2,256,128]{2,1,0:T(8,128)(2,1)S(1)}, bf16[2,256,128]{2,1,0:T(8,128)(2,1)S(1)}, u32[]{:S(2)}, u32[]{:S(2)}) collective-permute-start(bf16[2,256,128]{2,1,0:T(8,128)(2,1)S(1)} %bitcast.5), channel_id=1, source_target_pairs={{0,1},{1,0},{2,3},{3,2},{4,5},{5,4},{6,7},{7,6},{8,9},{9,8},{10,11... | collective-permute-start | bytes 393224 | tf_op jit(solution)/shard_map/ppermute | solution.py:152
  46.6 0.0 collective-permute-done.1.refs_2_
  46.6 4.2 %collective-permute-start.2 = (bf16[2,256,128]{2,1,0:T(8,128)(2,1)S(1)}, bf16[2,256,128]{2,1,0:T(8,128)(2,1)S(1)}, u32[]{:S(2)}, u32[]{:S(2)}) collective-permute-start(bf16[2,256,128]{2,1,0:T(8,128)(2,1)S(1)} %collective-permute-done.1.refs_2_), channel_id=1, source_target_pairs={{0,1},{1,0},{2,3},{3,2},{4,5},{5,4},{6,7},{7,6},{8,9},{9,8},{10,11... | collective-permute-start | bytes 393224 | tf_op jit(solution)/shard_map/ppermute | solution.py:153
  50.8 0.0 collective-permute-done.4.refs_6_
  50.8 0.0 collective-permute-done.refs_1_
  50.8 0.9 %collective-permute-done.2.refs_3_ = bf16[2,256,128]{2,1,0:T(8,128)(2,1)S(1)} collective-permute-done((bf16[2,256,128]{2,1,0:T(8,128)(2,1)S(1)}, bf16[2,256,128]{2,1,0:T(8,128)(2,1)S(1)}, u32[]{:S(2)}, u32[]{:S(2)}) %collective-permute-start.2) | collective-permute-done | bytes 131104 | tf_op jit(solution)/shard_map/ppermute | solution.py:153
  51.7 0.0 collective-permute-done.5.refs_7_
  51.7 0.0 copy-done
  51.7 4.4 %exchange_blocks.1 = bf16[8,256,128]{2,1,0:T(8,128)(2,1)S(1)} custom-call(bf16[2,256,128]{2,1,0:T(8,128)(2,1)S(1)} %bitcast.6, bf16[2,256,128]{2,1,0:T(8,128)(2,1)S(1)} %collective-permute-done.refs_1_, bf16[2,256,128]{2,1,0:T(8,128)(2,1)S(1)} %collective-permute-done.1.refs_2_, bf16[2,256,128]{2,1,0:T(8,128)(2,1)S(1)} %collective-permute-done.2.refs_3_, ...), custom_call_target="tpu_custom_call" | custom-call | tf_op jit(solution)/shard_map/exchange_blocks/pallas_call | solution.py:156
  56.1 30.0 %all_to_all.10.got = bf16[8,256,128]{2,1,0:T(8,128)(2,1)S(1)} all-to-all(bf16[8,256,128]{2,1,0:T(8,128)(2,1)S(1)} %exchange_blocks.1), channel_id=1, replica_groups=mesh['x'=8,'yh'=4,'yl'=2,'zh'=4,'zl'=2,'c'=2] {'yl','zh'}, dimensions={0} | all-to-all | bytes 1048576 | tf_op jit(solution)/shard_map/all_to_all | solution.py:172
  86.1 0.7 sum_slots.1
Async XLA Ops:
  0.7 37.8 %copy-start.1 = (s32[1,2]{1,0:T(1,128)S(1)}, s32[1,2]{1,0:T(1,128)}, u32[]{:S(2)}) copy-start(s32[1,2]{1,0:T(1,128)} %columns.1) | copy-start | bytes 28
  3.2 48.5 %copy-start = (bf16[2064,256]{1,0:T(8,128)(2,1)S(1)}, bf16[2064,256]{1,0:T(8,128)(2,1)}, u32[]{:S(2)}) copy-start(bf16[2064,256]{1,0:T(8,128)(2,1)} %get-tuple-element.8.refs_4_) | copy-start | bytes 3170308
  3.2 22.0 %collective-permute-start.3 = (bf16[2064,256]{1,0:T(8,128)(2,1)}, bf16[2064,256]{1,0:T(8,128)(2,1)S(1)}, u32[]{:S(2)}, u32[]{:S(2)}) collective-permute-start(bf16[2064,256]{1,0:T(8,128)(2,1)} %get-tuple-element.8.refs_4_), channel_id=1, source_target_pairs={{0,2},{2,0},{1,3},{3,1},{4,6},{6,4},{5,7},{7,5},{8,10},{10,8},{9,1... | collective-permute-start | bytes 3170312 | tf_op jit(solution)/shard_map/g_side/ppermute | solution.py:136
  9.1 29.4 %all-to-all-start = ((bf16[32,64,128]{2,1,0:T(8,128)(2,1)}), bf16[32,64,128]{2,1,0:T(8,128)(2,1)S(1)}, u32[]{:S(2)}, u32[]{:S(2)}) async-start(bf16[32,64,128]{2,1,0:T(8,128)(2,1)} %get-tuple-element.7), calls=%async_computation | async-start | bytes 1048576 | tf_op jit(solution)/shard_map/all_to_all | solution.py:141
  21.7 29.1 %collective-permute-start.4 = (bf16[2064,256]{1,0:T(8,128)(2,1)}, bf16[2064,256]{1,0:T(8,128)(2,1)}, u32[]{:S(2)}, u32[]{:S(2)}) collective-permute-start(bf16[2064,256]{1,0:T(8,128)(2,1)} %get-tuple-element.8.refs_4_), channel_id=1, source_target_pairs={{0,1},{1,0},{2,3},{3,2},{4,5},{5,4},{6,7},{7,6},{8,9},{9,8},{10,11... | collective-permute-start | bytes 3170312 | tf_op jit(solution)/shard_map/g_core/ppermute | solution.py:138
  25.3 26.5 %collective-permute-start.5 = (bf16[2064,256]{1,0:T(8,128)(2,1)S(1)}, bf16[2064,256]{1,0:T(8,128)(2,1)}, u32[]{:S(2)}, u32[]{:S(2)}) collective-permute-start(bf16[2064,256]{1,0:T(8,128)(2,1)S(1)} %collective-permute-done.3.refs_5_), channel_id=1, source_target_pairs={{0,1},{1,0},{2,3},{3,2},{4,5},{5,4},{6,7},{7,6},{8,9},{9,8},{10,11... | collective-permute-start | bytes 3170312 | tf_op jit(solution)/shard_map/g_both/ppermute | solution.py:140
  39.1 7.5 %collective-permute-start.1 = (bf16[2,256,128]{2,1,0:T(8,128)(2,1)S(1)}, bf16[2,256,128]{2,1,0:T(8,128)(2,1)S(1)}, u32[]{:S(2)}, u32[]{:S(2)}) collective-permute-start(bf16[2,256,128]{2,1,0:T(8,128)(2,1)S(1)} %bitcast.4), channel_id=1, source_target_pairs={{0,16},{16,0},{1,17},{17,1},{2,18},{18,2},{3,19},{19,3},{4,20},{20... | collective-permute-start | bytes 393224 | tf_op jit(solution)/shard_map/other/ppermute | solution.py:151
  41.0 9.8 %collective-permute-start = (bf16[2,256,128]{2,1,0:T(8,128)(2,1)S(1)}, bf16[2,256,128]{2,1,0:T(8,128)(2,1)S(1)}, u32[]{:S(2)}, u32[]{:S(2)}) collective-permute-start(bf16[2,256,128]{2,1,0:T(8,128)(2,1)S(1)} %bitcast.5), channel_id=1, source_target_pairs={{0,1},{1,0},{2,3},{3,2},{4,5},{5,4},{6,7},{7,6},{8,9},{9,8},{10,11... | collective-permute-start | bytes 393224 | tf_op jit(solution)/shard_map/ppermute | solution.py:152
  46.6 5.2 %collective-permute-start.2 = (bf16[2,256,128]{2,1,0:T(8,128)(2,1)S(1)}, bf16[2,256,128]{2,1,0:T(8,128)(2,1)S(1)}, u32[]{:S(2)}, u32[]{:S(2)}) collective-permute-start(bf16[2,256,128]{2,1,0:T(8,128)(2,1)S(1)} %collective-permute-done.1.refs_2_), channel_id=1, source_target_pairs={{0,1},{1,0},{2,3},{3,2},{4,5},{5,4},{6,7},{7,6},{8,9},{9,8},{10,11... | collective-permute-start | bytes 393224 | tf_op jit(solution)/shard_map/ppermute | solution.py:153

commit v7 on v6

--- a/solution.py
+++ b/solution.py
@@ -33,13 +33,14 @@
 
     rows, width = g_ref.shape
     packed[0:rows] = g_ref[...]
-    lane = lax.broadcasted_iota(jnp.int32, (TILE, width), 1)
-    listed = jnp.full((TILE, width), -1, jnp.int32)
+    lane = lax.broadcasted_iota(jnp.int32, (8, BLK), 1)
+    listed = jnp.full((8, BLK), -1, jnp.int32)
     for e in range(pairs.shape[2]):
         p = pairs[0, 0, e]
         here = jnp.where(e < count[0, 0], slots[0, p], -1)
         listed = jnp.where(lane == here, p, listed)
-    packed[rows:rows + TILE] = listed.astype(F32).astype(BF16)
+    listed = jnp.concatenate([listed.astype(F32)] * (TILE // 8), axis=0)
+    packed[rows:rows + TILE] = jnp.concatenate([listed] * (width // BLK), axis=1).astype(BF16)
 
 
 def exchange_kernel(*refs):

time: 88.4 us -> 88.4 us (level)
  no operation moved by 1% of the time
where the time goes in v7:
time: 88.4 us; the launch traced here: 86.8 us
  starting transfers between devices  44.8 us (51%)
  blocking collectives  30 us (34%)
  Pallas kernels  8.27 us (9%)
  waiting for transfers between devices  3.05 us (3%)
    all_to_all x1, blocking collectives, on_device(): arrived = lax.all_to_all(send, FAR, 0, 0, tiled=True)  30 us
    all_to_all x1, starting transfers between devices, on_device(): lax.all_to_all(mine, ORB, 0, 0, tiled=True)  12.6 us
    ppermute x1, starting transfers between devices, on_device(): g_both = lax.ppermute(g_side, 'c', SWAP)  11.1 us
    ppermute x1, starting transfers between devices, on_device(): g_side = lax.ppermute(g, 'zl', SWAP)  5.86 us
    ppermute x1, starting transfers between devices, on_device(): own_far = lax.ppermute(own, 'c', SWAP)  5.55 us
    pallas_call x1, Pallas kernels, on_device(): pl.pallas_call(exchange_kernel, out_shape=jax.ShapeDtypeStruct((n_far, OW...  4.41 us
    ppermute x1, starting transfers between devices, on_device(): coeffs = (own, own_far, other, lax.ppermute(other, 'c', SWAP))  4.18 us
    ppermute x1, starting transfers between devices, on_device(): g_core = lax.ppermute(g, 'c', SWAP)  3.55 us
  transfers between devices with their start and end apart: 7, of which 2 were waited for; matrix products, arithmetic and copies ran while one was open for 0% of the time, Pallas kernels for 1%

profile of v7, /device:TPU:1, one launch (start us, length us, event | category | flops | bytes accessed | tf_op | source)
XLA Modules:
  0.0 86.8 jit_solution(9697399365805876695)
XLA Ops:
  0.7 0.0 copy-start.1
  0.7 2.6 %prepare.1 = (bf16[32,64,128]{2,1,0:T(8,128)(2,1)}, bf16[2064,256]{1,0:T(8,128)(2,1)}) custom-call(s32[1,1,32]{2,1,0:T(1,128)} %pairs.1, s32[1,1]{1,0:T(1,128)S(6)} %copy.8.count, s32[1,64]{1,0:T(1,128)} %slots.1, bf16[16,1024]{1,0:T(8,128)(2,1)} %occ.1, bf16[16,1024]{1,0:T(8,128)(2,1)} %amp.1, bf16[2048,256]{1,0:T(8,128)(2,1)} %bitcast.7), custom_call_target="tpu_custom_call" | custom-call | tf_op jit(solution)/shard_map/prepare/pallas_call | solution.py:126
  3.2 0.0 copy-start
  3.2 5.9 %collective-permute-start.3 = (bf16[2064,256]{1,0:T(8,128)(2,1)}, bf16[2064,256]{1,0:T(8,128)(2,1)S(1)}, u32[]{:S(2)}, u32[]{:S(2)}) collective-permute-start(bf16[2064,256]{1,0:T(8,128)(2,1)} %get-tuple-element.8.refs_4_), channel_id=1, source_target_pairs={{0,2},{2,0},{1,3},{3,1},{4,6},{6,4},{5,7},{7,5},{8,10},{10,8},{9,1... | collective-permute-start | bytes 3170312 | tf_op jit(solution)/shard_map/g_side/ppermute | solution.py:137
  9.1 12.6 %all-to-all-start = ((bf16[32,64,128]{2,1,0:T(8,128)(2,1)}), bf16[32,64,128]{2,1,0:T(8,128)(2,1)S(1)}, u32[]{:S(2)}, u32[]{:S(2)}) async-start(bf16[32,64,128]{2,1,0:T(8,128)(2,1)} %get-tuple-element.7), calls=%async_computation | async-start | bytes 1048576 | tf_op jit(solution)/shard_map/all_to_all | solution.py:142
  21.7 3.5 %collective-permute-start.4 = (bf16[2064,256]{1,0:T(8,128)(2,1)}, bf16[2064,256]{1,0:T(8,128)(2,1)}, u32[]{:S(2)}, u32[]{:S(2)}) collective-permute-start(bf16[2064,256]{1,0:T(8,128)(2,1)} %get-tuple-element.8.refs_4_), channel_id=1, source_target_pairs={{0,1},{1,0},{2,3},{3,2},{4,5},{5,4},{6,7},{7,6},{8,9},{9,8},{10,11... | collective-permute-start | bytes 3170312 | tf_op jit(solution)/shard_map/g_core/ppermute | solution.py:139
  25.2 0.0 collective-permute-done.3.refs_5_
  25.3 11.1 %collective-permute-start.5 = (bf16[2064,256]{1,0:T(8,128)(2,1)S(1)}, bf16[2064,256]{1,0:T(8,128)(2,1)}, u32[]{:S(2)}, u32[]{:S(2)}) collective-permute-start(bf16[2064,256]{1,0:T(8,128)(2,1)S(1)} %collective-permute-done.3.refs_5_), channel_id=1, source_target_pairs={{0,1},{1,0},{2,3},{3,2},{4,5},{5,4},{6,7},{7,6},{8,9},{9,8},{10,11... | collective-permute-start | bytes 3170312 | tf_op jit(solution)/shard_map/g_both/ppermute | solution.py:141
  36.4 2.1 %all-to-all-done = bf16[32,64,128]{2,1,0:T(8,128)(2,1)S(1)} async-done(((bf16[32,64,128]{2,1,0:T(8,128)(2,1)}), bf16[32,64,128]{2,1,0:T(8,128)(2,1)S(1)}, u32[]{:S(2)}, u32[]{:S(2)}) %all-to-all-start) | async-done | bytes 524320 | tf_op jit(solution)/shard_map/all_to_all | solution.py:142
  38.5 0.0 copy-done.1
  38.5 0.6 select_columns.1
  39.1 1.9 %collective-permute-start.1 = (bf16[2,256,128]{2,1,0:T(8,128)(2,1)S(1)}, bf16[2,256,128]{2,1,0:T(8,128)(2,1)S(1)}, u32[]{:S(2)}, u32[]{:S(2)}) collective-permute-start(bf16[2,256,128]{2,1,0:T(8,128)(2,1)S(1)} %bitcast.4), channel_id=1, source_target_pairs={{0,16},{16,0},{1,17},{17,1},{2,18},{18,2},{3,19},{19,3},{4,20},{20... | collective-permute-start | bytes 393224 | tf_op jit(solution)/shard_map/other/ppermute | solution.py:152
  41.0 5.6 %collective-permute-start = (bf16[2,256,128]{2,1,0:T(8,128)(2,1)S(1)}, bf16[2,256,128]{2,1,0:T(8,128)(2,1)S(1)}, u32[]{:S(2)}, u32[]{:S(2)}) collective-permute-start(bf16[2,256,128]{2,1,0:T(8,128)(2,1)S(1)} %bitcast.5), channel_id=1, source_target_pairs={{0,1},{1,0},{2,3},{3,2},{4,5},{5,4},{6,7},{7,6},{8,9},{9,8},{10,11... | collective-permute-start | bytes 393224 | tf_op jit(solution)/shard_map/ppermute | solution.py:153
  46.6 0.0 collective-permute-done.1.refs_2_
  46.6 4.2 %collective-permute-start.2 = (bf16[2,256,128]{2,1,0:T(8,128)(2,1)S(1)}, bf16[2,256,128]{2,1,0:T(8,128)(2,1)S(1)}, u32[]{:S(2)}, u32[]{:S(2)}) collective-permute-start(bf16[2,256,128]{2,1,0:T(8,128)(2,1)S(1)} %collective-permute-done.1.refs_2_), channel_id=1, source_target_pairs={{0,1},{1,0},{2,3},{3,2},{4,5},{5,4},{6,7},{7,6},{8,9},{9,8},{10,11... | collective-permute-start | bytes 393224 | tf_op jit(solution)/shard_map/ppermute | solution.py:154
  50.8 0.0 collective-permute-done.4.refs_6_
  50.8 0.0 collective-permute-done.refs_1_
  50.8 0.9 %collective-permute-done.2.refs_3_ = bf16[2,256,128]{2,1,0:T(8,128)(2,1)S(1)} collective-permute-done((bf16[2,256,128]{2,1,0:T(8,128)(2,1)S(1)}, bf16[2,256,128]{2,1,0:T(8,128)(2,1)S(1)}, u32[]{:S(2)}, u32[]{:S(2)}) %collective-permute-start.2) | collective-permute-done | bytes 131104 | tf_op jit(solution)/shard_map/ppermute | solution.py:154
  51.7 0.0 collective-permute-done.5.refs_7_
  51.7 0.0 copy-done
  51.7 4.4 %exchange_blocks.1 = bf16[8,256,128]{2,1,0:T(8,128)(2,1)S(1)} custom-call(bf16[2,256,128]{2,1,0:T(8,128)(2,1)S(1)} %bitcast.6, bf16[2,256,128]{2,1,0:T(8,128)(2,1)S(1)} %collective-permute-done.refs_1_, bf16[2,256,128]{2,1,0:T(8,128)(2,1)S(1)} %collective-permute-done.1.refs_2_, bf16[2,256,128]{2,1,0:T(8,128)(2,1)S(1)} %collective-permute-done.2.refs_3_, ...), custom_call_target="tpu_custom_call" | custom-call | tf_op jit(solution)/shard_map/exchange_blocks/pallas_call | solution.py:157
  56.1 30.0 %all_to_all.10.got = bf16[8,256,128]{2,1,0:T(8,128)(2,1)S(1)} all-to-all(bf16[8,256,128]{2,1,0:T(8,128)(2,1)S(1)} %exchange_blocks.1), channel_id=1, replica_groups=mesh['x'=8,'yh'=4,'yl'=2,'zh'=4,'zl'=2,'c'=2] {'yl','zh'}, dimensions={0} | all-to-all | bytes 1048576 | tf_op jit(solution)/shard_map/all_to_all | solution.py:173
  86.1 0.7 sum_slots.1
Async XLA Ops:
  0.7 37.8 %copy-start.1 = (s32[1,2]{1,0:T(1,128)S(1)}, s32[1,2]{1,0:T(1,128)}, u32[]{:S(2)}) copy-start(s32[1,2]{1,0:T(1,128)} %columns.1) | copy-start | bytes 28
  3.2 48.5 %copy-start = (bf16[2064,256]{1,0:T(8,128)(2,1)S(1)}, bf16[2064,256]{1,0:T(8,128)(2,1)}, u32[]{:S(2)}) copy-start(bf16[2064,256]{1,0:T(8,128)(2,1)} %get-tuple-element.8.refs_4_) | copy-start | bytes 3170308
  3.2 22.0 %collective-permute-start.3 = (bf16[2064,256]{1,0:T(8,128)(2,1)}, bf16[2064,256]{1,0:T(8,128)(2,1)S(1)}, u32[]{:S(2)}, u32[]{:S(2)}) collective-permute-start(bf16[2064,256]{1,0:T(8,128)(2,1)} %get-tuple-element.8.refs_4_), channel_id=1, source_target_pairs={{0,2},{2,0},{1,3},{3,1},{4,6},{6,4},{5,7},{7,5},{8,10},{10,8},{9,1... | collective-permute-start | bytes 3170312 | tf_op jit(solution)/shard_map/g_side/ppermute | solution.py:137
  9.1 29.4 %all-to-all-start = ((bf16[32,64,128]{2,1,0:T(8,128)(2,1)}), bf16[32,64,128]{2,1,0:T(8,128)(2,1)S(1)}, u32[]{:S(2)}, u32[]{:S(2)}) async-start(bf16[32,64,128]{2,1,0:T(8,128)(2,1)} %get-tuple-element.7), calls=%async_computation | async-start | bytes 1048576 | tf_op jit(solution)/shard_map/all_to_all | solution.py:142
  21.7 29.1 %collective-permute-start.4 = (bf16[2064,256]{1,0:T(8,128)(2,1)}, bf16[2064,256]{1,0:T(8,128)(2,1)}, u32[]{:S(2)}, u32[]{:S(2)}) collective-permute-start(bf16[2064,256]{1,0:T(8,128)(2,1)} %get-tuple-element.8.refs_4_), channel_id=1, source_target_pairs={{0,1},{1,0},{2,3},{3,2},{4,5},{5,4},{6,7},{7,6},{8,9},{9,8},{10,11... | collective-permute-start | bytes 3170312 | tf_op jit(solution)/shard_map/g_core/ppermute | solution.py:139
  25.3 26.5 %collective-permute-start.5 = (bf16[2064,256]{1,0:T(8,128)(2,1)S(1)}, bf16[2064,256]{1,0:T(8,128)(2,1)}, u32[]{:S(2)}, u32[]{:S(2)}) collective-permute-start(bf16[2064,256]{1,0:T(8,128)(2,1)S(1)} %collective-permute-done.3.refs_5_), channel_id=1, source_target_pairs={{0,1},{1,0},{2,3},{3,2},{4,5},{5,4},{6,7},{7,6},{8,9},{9,8},{10,11... | collective-permute-start | bytes 3170312 | tf_op jit(solution)/shard_map/g_both/ppermute | solution.py:141
  39.1 7.5 %collective-permute-start.1 = (bf16[2,256,128]{2,1,0:T(8,128)(2,1)S(1)}, bf16[2,256,128]{2,1,0:T(8,128)(2,1)S(1)}, u32[]{:S(2)}, u32[]{:S(2)}) collective-permute-start(bf16[2,256,128]{2,1,0:T(8,128)(2,1)S(1)} %bitcast.4), channel_id=1, source_target_pairs={{0,16},{16,0},{1,17},{17,1},{2,18},{18,2},{3,19},{19,3},{4,20},{20... | collective-permute-start | bytes 393224 | tf_op jit(solution)/shard_map/other/ppermute | solution.py:152
  41.0 9.8 %collective-permute-start = (bf16[2,256,128]{2,1,0:T(8,128)(2,1)S(1)}, bf16[2,256,128]{2,1,0:T(8,128)(2,1)S(1)}, u32[]{:S(2)}, u32[]{:S(2)}) collective-permute-start(bf16[2,256,128]{2,1,0:T(8,128)(2,1)S(1)} %bitcast.5), channel_id=1, source_target_pairs={{0,1},{1,0},{2,3},{3,2},{4,5},{5,4},{6,7},{7,6},{8,9},{9,8},{10,11... | collective-permute-start | bytes 393224 | tf_op jit(solution)/shard_map/ppermute | solution.py:153
  46.6 5.2 %collective-permute-start.2 = (bf16[2,256,128]{2,1,0:T(8,128)(2,1)S(1)}, bf16[2,256,128]{2,1,0:T(8,128)(2,1)S(1)}, u32[]{:S(2)}, u32[]{:S(2)}) collective-permute-start(bf16[2,256,128]{2,1,0:T(8,128)(2,1)S(1)} %collective-permute-done.1.refs_2_), channel_id=1, source_target_pairs={{0,1},{1,0},{2,3},{3,2},{4,5},{5,4},{6,7},{7,6},{8,9},{9,8},{10,11... | collective-permute-start | bytes 393224 | tf_op jit(solution)/shard_map/ppermute | solution.py:154
